TPU v7x, 32 devices: a whole 2x2x4 slice. The times are simulated.
32 devices in a mesh: fsdp: 8 (over z, x), tp: 4 (over y, core).
Axes of the slice: x: 2, y: 2, z: 4, core: 2. Of those that a mesh axis runs over, the one named last changes fastest.
Arguments:
- hidden: bfloat16 [2048, 14336], P('fsdp', 'tp'), may hold values from -6 to 6
- cotangent: bfloat16 [2048, 5120], P('fsdp'), may hold values from -6 to 6
- weight: bfloat16 [14336, 5120], P('tp', 'fsdp'), may hold values from -0.046875 to 0.046875
- prompt_hidden: bfloat16 [1024, 14336], P('fsdp', 'tp'), may hold values from -6 to 6
Outputs:
- grad_hidden: bfloat16 [2048, 14336], P('fsdp', 'tp')
- new_weight: bfloat16 [14336, 5120], P('tp', 'fsdp')
- prompt_out: bfloat16 [1024, 5120], P('fsdp')
All inputs are finite; a program needn't handle non-finite values.
Results may differ from a plain program's by a relative error of at most 0.014.
Values may be sent and summed in bfloat16 or wider, within the bound.
A program may use at most 192 MiB of HBM per device.

v0:
```python
import math

import jax
import jax.numpy as jnp
from jax import lax
from jax.sharding import PartitionSpec as P

FH = 14336


def body(hidden, cotangent, weight, prompt_hidden):
    width_local = weight.shape[1]
    fsdp_count = lax.axis_size("fsdp")
    factor = 0.5 / math.sqrt(hidden.shape[0] * fsdp_count * FH)
    all_hidden = lax.all_gather(hidden, "fsdp", axis=0, tiled=True)
    all_cotangent = lax.all_to_all(cotangent, "fsdp", split_axis=1, concat_axis=0, tiled=True)
    grouped_hidden = all_hidden.reshape(fsdp_count, hidden.shape[0], hidden.shape[1])
    grouped_cot = all_cotangent.reshape(fsdp_count, hidden.shape[0], width_local)
    parts = jnp.einsum(
        "gtf,gtd->gfd", grouped_hidden, grouped_cot, preferred_element_type=jnp.float32
    )
    grad_weight = jnp.sum(parts.astype(jnp.bfloat16).astype(jnp.float32), axis=0)
    feature_terms = lax.dot_general(
        all_cotangent, weight, (((1,), (1,)), ((), ())), preferred_element_type=jnp.float32
    )
    grad_hidden = lax.psum_scatter(
        feature_terms.astype(jnp.bfloat16), "fsdp", scatter_dimension=0, tiled=True
    )
    new_weight = (weight.astype(jnp.float32) - factor * grad_weight).astype(jnp.bfloat16)
    partial_out = jnp.dot(
        prompt_hidden,
        lax.all_gather(new_weight, "fsdp", axis=1, tiled=True),
        preferred_element_type=jnp.float32,
    )
    prompt_out = lax.psum(partial_out.astype(jnp.bfloat16), "tp")
    return (grad_hidden, new_weight, prompt_out)


def solution(mesh):
    placed = (P("fsdp", "tp"), P("fsdp", None), P("tp", "fsdp"), P("fsdp", "tp"))
    return jax.shard_map(
        body,
        mesh=mesh,
        in_specs=placed,
        out_specs=(P("fsdp", "tp"), P("tp", "fsdp"), P("fsdp", None)),
        check_vma=False,
    )
```

profile of v0, /device:TPU:0, one launch (start us, length us, event | category | flops | bytes accessed | tf_op | source)
XLA Modules:
  0.0 1296.6 jit_solution(3764038899883590500)
XLA Ops:
  7.2 0.0 copy-start
  7.2 0.0 all-gather.3.cloned.1.call-start
  7.2 0.7 all-gather.3.cloned.1.call-update
  7.9 0.0 all-gather.5.cloned.1.call-start
  8.0 4.4 copy.8
  12.3 3.1 copy.9
  15.5 124.2 %all_to_all.19 = bf16[256,8,640]{2,0,1:T(8,128)(2,1)} all-to-all(bf16[256,8,640]{2,0,1:T(8,128)(2,1)S(1)} %copy.9), channel_id=1, replica_groups=mesh['fsdp'=8,'tp'=4] {'fsdp'}, dimensions={1} | all-to-all | bytes 5242880 | tf_op jit(solution)/shard_map/all_to_all | solution.py:16
  139.6 130.4 %all-gather.3.cloned.1.call-done = bf16[2048,3584]{1,0:T(8,128)(2,1)} async-done(((bf16[256,3584]{1,0:T(8,128)(2,1)}), bf16[2048,3584]{1,0:T(8,128)(2,1)}) %all-gather.3.cloned.1.call-update) | async-done | bytes 14680080 | tf_op jit(solution)/shard_map/all_gather | solution.py:15
  270.0 19.3 %convert_reduce_fusion = f32[3584,640]{1,0:T(8,128)} fusion(bf16[8,256,3584]{2,1,0:T(8,128)(2,1)} %bitcast.16, bf16[256,8,640]{2,0,1:T(8,128)(2,1)} %all_to_all.19), kind=kOutput, calls=%fused_computation | convolution fusion | flops 9447997440 | bytes 26476544 | tf_op jit(solution)/shard_map/gtf,gtd->gfd/dot_general | solution.py:19
  289.3 8.3 subtract_convert_fusion
  297.6 0.0 all-gather.5.cloned.1.call-update
  297.6 0.0 copy-start.2
  297.6 0.0 all-reduce.2.cloned.1.call-start
  297.6 695.0 %all-gather.5.cloned.1.call-done = bf16[3584,5120]{1,0:T(8,128)(2,1)} async-done(((bf16[3584,640]{1,0:T(8,128)(2,1)}), bf16[3584,5120]{1,0:T(8,128)(2,1)}) %all-gather.5.cloned.1.call-update) | async-done | bytes 36700176 | tf_op jit(solution)/shard_map/all_gather | solution.py:32
  992.6 0.0 copy-done
  992.6 17.7 %fusion = bf16[128,5120]{0,1:T(8,128)(2,1)} fusion(bf16[3584,5120]{1,0:T(8,128)(2,1)} %all-gather.5.cloned.1.call-done, bf16[128,3584]{1,0:T(8,128)(2,1)S(1)} %copy-done), kind=kOutput, calls=%fused_computation.4 | convolution fusion | flops 4698275840 | bytes 38928384 | tf_op jit(solution)/shard_map/dot_general | solution.py:30
  1010.3 0.0 all-reduce.2.cloned.1.call-update
  1010.3 0.2 reduce-scatter.2.cloned.1.call-start
  1010.6 0.0 copy-done.2
  1010.6 16.7 %convolution_convert_fusion = bf16[2048,3584]{1,0:T(8,128)(2,1)} fusion(bf16[2048,640]{1,0:T(8,128)(2,1)S(1)} %bitcast.15, bf16[3584,640]{1,0:T(8,128)(2,1)} %param.6), kind=kOutput, calls=%fused_computation.1 | convolution fusion | flops 9402580992 | bytes 21889024 | tf_op jit(solution)/shard_map/dot_general | solution.py:23
  1027.3 0.0 reduce-scatter.2.cloned.1.call-update
  1027.3 0.0 copy-start.1
  1027.3 22.1 %all-reduce.2.cloned.1.call-done = bf16[128,5120]{0,1:T(8,128)(2,1)} async-done(((bf16[128,5120]{0,1:T(8,128)(2,1)}), bf16[128,5120]{0,1:T(8,128)(2,1)}) %all-reduce.2.cloned.1.call-update) | async-done | bytes 1310736 | tf_op jit(solution)/shard_map/psum | solution.py:35
  1049.4 2.4 copy.11
  1051.8 238.2 %reduce-scatter.2.cloned.1.call-done = bf16[256,3584]{1,0:T(8,128)(2,1)} async-done(((bf16[2048,3584]{1,0:T(8,128)(2,1)}), bf16[256,3584]{1,0:T(8,128)(2,1)}) %reduce-scatter.2.cloned.1.call-update) | async-done | bytes 1835024 | tf_op jit(solution)/shard_map/reduce_scatter | solution.py:26
  1290.0 0.0 copy-done.1
Async XLA Ops:
  7.2 985.5 %copy-start = (bf16[128,3584]{1,0:T(8,128)(2,1)S(1)}, bf16[128,3584]{1,0:T(8,128)(2,1)}, u32[]{:S(2)}) copy-start(bf16[128,3584]{1,0:T(8,128)(2,1)} %param.7) | copy-start | bytes 2752516
  7.2 262.8 %all-gather.3.cloned.1.call-start = ((), (), s32[]{:S(2)}) async-start(), calls=%async_computation.3 | async-start | bytes 16515072 | tf_op jit(solution)/shard_map/all_gather | solution.py:15
  7.9 984.7 %all-gather.5.cloned.1.call-start = ((), (), s32[]{:S(2)}) async-start(), calls=%async_computation.4 | async-start | bytes 41287680 | tf_op jit(solution)/shard_map/all_gather | solution.py:32
  297.6 713.0 %copy-start.2 = (bf16[256,8,640]{2,0,1:T(8,128)(2,1)S(1)}, bf16[256,8,640]{2,0,1:T(8,128)(2,1)}, u32[]{:S(2)}) copy-start(bf16[256,8,640]{2,0,1:T(8,128)(2,1)} %all_to_all.19) | copy-start | bytes 7864324
  297.6 751.8 %all-reduce.2.cloned.1.call-start = ((), (), s32[]{:S(2)}) async-start(), calls=%async_computation.5 | async-start | bytes 2621440 | tf_op jit(solution)/shard_map/psum | solution.py:35
  1010.3 279.7 %reduce-scatter.2.cloned.1.call-start = ((), (), s32[]{:S(2)}) async-start(), calls=%async_computation.2 | async-start | bytes 16515072 | tf_op jit(solution)/shard_map/reduce_scatter | solution.py:26
  1027.3 262.7 %copy-start.1 = (bf16[128,3584]{1,0:T(8,128)(2,1)S(1)}, bf16[128,3584]{1,0:T(8,128)(2,1)}, u32[]{:S(2)}) copy-start(bf16[128,3584]{1,0:T(8,128)(2,1)} %param.7) | copy-start | bytes 2752516
Sparse Core Ops, SparseCore 0:
  10.2 259.7 all-gather.2
  297.7 694.8 all-gather.4
  1010.5 38.9 all-reduce.1
  1053.4 236.5 reduce-scatter.1
where the time goes:
time: 1300 us
  waiting for transfers between devices  1090 us (84%)
  blocking collectives  124 us (10%)
  matrix products  53.7 us (4%)
  between operations  13.8 us (1%)
    all_gather x1, waiting for transfers between devices, body(): lax.all_gather(new_weight, 'fsdp', axis=1, tiled=True)  695 us
    reduce_scatter x1, waiting for transfers between devices, body(): lax.psum_scatter(feature_terms.astype(jnp.bfloat16), 'fsdp', scatter_dime...  238 us
    all_gather x1, waiting for transfers between devices, body(): all_hidden = lax.all_gather(hidden, 'fsdp', axis=0, tiled=True)  130 us
    all_to_all x1, blocking collectives, body(): lax.all_to_all(cotangent, 'fsdp', split_axis=1, concat_axis=0, tiled=True)  124 us
  transfers between devices with their start and end apart: 4, of which 4 were waited for; matrix products, arithmetic and copies ran while one was open for 2% of the time, Pallas kernels for 0%

commit v1 on v0

v1 whole, which is shorter than its diff:
```python
import math

import jax
import jax.numpy as jnp
from jax import lax
from jax.sharding import PartitionSpec as P

F32, BF16 = jnp.float32, jnp.bfloat16


def block_of(blocks, index):
    return lax.dynamic_index_in_dim(blocks, index, 0, keepdims=False)


def swap_blocks(blocks, axis, stride=1):
    count = lax.axis_size(axis)
    groups = count // stride
    me = lax.axis_index(axis) // stride
    got = [block_of(blocks, me)]
    for k in range(1, groups):
        perm = [(i, (i + k * stride) % count) for i in range(count)]
        got.append(lax.ppermute(block_of(blocks, (me + k) % groups), axis, perm))
    return got


def in_order(items, index):
    count = len(items)
    twice = jnp.stack(items[::-1] * 2)
    return lax.dynamic_slice_in_dim(twice, (count - 1 - index) % count, count, 0)


def gather_by_permutes(block, axis):
    count = lax.axis_size(axis)
    items = [block]
    for k in range(1, count):
        items.append(lax.ppermute(block, axis, [(i, (i + k) % count) for i in range(count)]))
    return in_order(items, lax.axis_index(axis))


def line_gather(block, line, step_of):
    length, at = line
    up, down = [block], [block]
    for k in range(1, length):
        up.append(lax.ppermute(up[-1], "fsdp", step_of(range(k - 1, length - 1), 1)))
        down.append(lax.ppermute(down[-1], "fsdp", step_of(range(1, length - k + 1), -1)))
    return [block] + [
        jnp.where(at >= k, up[k], down[length - k]) for k in range(1, length)
    ]


def body(hidden, cotangent, weight, prompt_hidden):
    tokens, units = hidden.shape
    width = weight.shape[1]
    prompts = prompt_hidden.shape[0]
    n_fsdp, n_tp = lax.axis_size("fsdp"), lax.axis_size("tp")
    length = n_fsdp // 2
    me = lax.axis_index("fsdp")
    tp = lax.axis_index("tp")
    z, x = me // 2, me % 2
    factor = 0.5 / math.sqrt(tokens * n_fsdp * units * n_tp)
    across = [(i, i ^ 1) for i in range(n_fsdp)]

    def step_of(froms, by):
        return [(2 * a + b, 2 * (a + by) + b) for a in froms for b in range(2)]

    part = tokens // n_tp
    rows = lax.dynamic_slice_in_dim(cotangent, tp * part, part, 0)
    rows = rows.reshape(part, length, 2 * width).transpose(1, 0, 2)
    mine = jnp.stack(swap_blocks(rows, "fsdp", 2))
    cot = gather_by_permutes(mine, "tp")
    cot = cot.transpose(1, 0, 2, 3).reshape(length, tokens, 2 * width)
    cot_first = cot[:, :, :width]
    cot_second = cot[:, :, width:]
    cot_own = jnp.where(x == 0, cot_first, cot_second)
    cot_peer = jnp.where(x == 0, cot_second, cot_first)

    weight_peer = lax.ppermute(weight, "fsdp", across)
    line_hidden = line_gather(hidden, (length, z), step_of)

    both = jnp.concatenate([weight, weight_peer], axis=1)
    cot_both = jnp.concatenate([cot_own, cot_peer], axis=2)
    terms = [
        lax.dot_general(cot_both[k], both, (((1,), (1,)), ((), ())), preferred_element_type=F32)
        for k in range(length)
    ]
    up = down = None
    for s in range(1, length):
        send_up, send_down = terms[s], terms[length - s]
        if s > 1:
            send_up = send_up + up.astype(F32)
            send_down = send_down + down.astype(F32)
        up = lax.ppermute(send_up.astype(BF16), "fsdp", step_of(range(0, s), 1))
        down = lax.ppermute(
            send_down.astype(BF16), "fsdp", step_of(range(length - s, length), -1)
        )
    grad_hidden = (terms[0] + up.astype(F32) + down.astype(F32)).astype(BF16)

    grouped = jnp.stack(line_hidden)

    def gradient(cots):
        parts = jnp.einsum("gtf,gtd->gfd", grouped, cots, preferred_element_type=F32)
        return jnp.sum(parts.astype(BF16).astype(F32), axis=0)

    other = lax.ppermute(gradient(cot_peer).astype(BF16), "fsdp", across)
    grad_weight = gradient(cot_own) + other.astype(F32)
    new_weight = (weight.astype(F32) - factor * grad_weight).astype(BF16)

    line_prompt = jnp.stack(line_gather(prompt_hidden, (length, z), step_of))
    pair_prompt = lax.ppermute(line_prompt, "fsdp", across)
    all_prompt = jnp.stack([line_prompt, pair_prompt])
    share = lax.dot_general(
        all_prompt.reshape(n_fsdp * prompts, units), new_weight,
        (((1,), (0,)), ((), ())), preferred_element_type=F32,
    ).astype(BF16)
    piece = prompts // n_tp
    share = share.reshape(n_fsdp, n_tp, piece, width).transpose(1, 0, 2, 3)
    shares = swap_blocks(share, "tp")
    summed = sum(s.astype(F32) for s in shares).astype(BF16)
    summed = summed.reshape(2, length, piece, width)
    pieces = []
    for a in range(2):
        for k in range(length):
            if a == k == 0:
                pieces.append(summed[0, 0])
            else:
                perm = [
                    (i, 2 * ((i // 2 - k) % length) + ((i % 2) ^ a)) for i in range(n_fsdp)
                ]
                pieces.append(lax.ppermute(summed[a, k], "fsdp", perm))
    columns = jnp.stack(pieces).reshape(2, length, piece, width)
    columns = jnp.where(x == 0, columns, columns[::-1])
    columns = jnp.concatenate([columns, columns], axis=1)
    columns = lax.dynamic_slice_in_dim(columns, (length - z) % length, length, 1)
    out_rows = columns.transpose(2, 1, 0, 3).reshape(piece, n_fsdp * width)
    prompt_out = gather_by_permutes(out_rows, "tp").reshape(prompts, n_fsdp * width)
    return (grad_hidden, new_weight, prompt_out)


def solution(mesh):
    placed = (P("fsdp", "tp"), P("fsdp", None), P("tp", "fsdp"), P("fsdp", "tp"))
    return jax.shard_map(
        body,
        mesh=mesh,
        in_specs=placed,
        out_specs=(P("fsdp", "tp"), P("tp", "fsdp"), P("fsdp", None)),
        check_vma=False,
    )
```

time: 1300 us -> 554 us (0.43)
  waiting for transfers between devices: 1090 us -> 366 us
  blocking collectives: 124 us -> 0 us
  starting transfers between devices: 0.34 us -> 64.9 us
  other arithmetic: 8.26 us -> 33.8 us
  local copies, waits for them, and re-layouts: 9.95 us -> 24.8 us
    all_gather x2 -> x0, waiting for transfers between devices: 825 us -> none  [the longest x1 695 us: body(): lax.all_gather(new_weight, 'fsdp', axis=1, tiled=True)]
    ppermute x0 -> x40, waiting for transfers between devices: none -> 366 us  [the longest x6 116 us: line_gather(): lax.ppermute(down[-1], 'fsdp', step_of(range(1, length - k + 1), -1))]
    reduce_scatter x1 -> x0, waiting for transfers between devices: 238 us -> none  [body(): lax.psum_scatter(feature_terms.astype(jnp.bfloat16), 'fsdp', scatter_dime...]
    all_to_all x1 -> x0, blocking collectives: 124 us -> none  [body(): lax.all_to_all(cotangent, 'fsdp', split_axis=1, concat_axis=0, tiled=True)]
    ppermute x0 -> x40, starting transfers between devices: none -> 64.9 us  [the longest x7 14.8 us: body(): pieces.append(lax.ppermute(summed[a, k], 'fsdp', perm))]
    psum x1 -> x0, waiting for transfers between devices: 22.1 us -> none  [body(): prompt_out = lax.psum(partial_out.astype(jnp.bfloat16), 'tp')]
    another operation x0 -> x10, other arithmetic: none -> 14.5 us  [the longest x2 7.97 us: body(): all_prompt = jnp.stack([line_prompt, pair_prompt])]
    dot_general x3 -> x7, matrix products: 53.7 us -> 61.7 us  [the longest x4 28.4 us: body(): lax.dot_general(cot_both[k], both, (((1,), (1,)), ((), ())), preferred_el...]
  transfers between devices with their start and end apart: 4 -> 40, of which waited for: 4 -> 19; matrix products, arithmetic and copies ran while one was open for 2% -> 19% of each run, Pallas kernels for 0% -> 0%
where the time goes in v1:
time: 554 us; the launch traced here: 553 us
  waiting for transfers between devices  366 us (66%)
  starting transfers between devices  64.9 us (12%)
  matrix products  61.7 us (11%)
  other arithmetic  33.8 us (6%)
  local copies, waits for them, and re-layouts  24.8 us (4%)
    ppermute x6, waiting for transfers between devices, line_gather(): lax.ppermute(down[-1], 'fsdp', step_of(range(1, length - k + 1), -1))  116 us
    ppermute x3, waiting for transfers between devices, body(): lax.ppermute(send_down.astype(BF16), 'fsdp', step_of(range(length - s, le...  68.1 us
    ppermute x1, waiting for transfers between devices, body(): other = lax.ppermute(gradient(cot_peer).astype(BF16), 'fsdp', across)  55.3 us
    ppermute x7, waiting for transfers between devices, body(): pieces.append(lax.ppermute(summed[a, k], 'fsdp', perm))  38.1 us
    ppermute x6, waiting for transfers between devices, line_gather(): lax.ppermute(up[-1], 'fsdp', step_of(range(k - 1, length - 1), 1))  30.4 us
    dot_general x4, matrix products, body(): lax.dot_general(cot_both[k], both, (((1,), (1,)), ((), ())), preferred_el...  28.4 us
    ppermute x6, waiting for transfers between devices, gather_by_permutes(): lax.ppermute(block, axis, [(i, (i + k) % count) for i in range(count)])  24.7 us
    dot_general x2, matrix products, gradient(): jnp.einsum('gtf,gtd->gfd', grouped, cots, preferred_element_type=F32)  23.7 us
  transfers between devices with their start and end apart: 40, of which 19 were waited for; matrix products, arithmetic and copies ran while one was open for 19% of the time, Pallas kernels for 0%

profile of v1, /device:TPU:0, one launch (start us, length us, event | category | flops | bytes accessed | tf_op | source)
XLA Modules:
  0.0 553.0 jit_solution(8691841763733156318)
XLA Ops:
  0.7 1.7 copy-done
  2.9 1.4 constant_dynamic-slice_fusion.4
  4.3 5.1 collective-permute-start.2
  9.6 1.0 collective-permute-start
  10.6 3.4 collective-permute-done.2
  14.1 9.2 %collective-permute-done.1 = bf16[64,1280]{1,0:T(8,128)(2,1)S(1)} collective-permute-done((bf16[64,1280]{1,0:T(8,128)(2,1)S(1)}, bf16[64,1280]{1,0:T(8,128)(2,1)S(1)}, u32[]{:S(2)}, u32[]{:S(2)}) %collective-permute-start.1) | collective-permute-done | bytes 163872 | tf_op jit(solution)/shard_map/ppermute | solution.py:22
  24.9 3.8 copy.24
  28.7 4.0 collective-permute-start.13
  32.7 1.3 collective-permute-start.14
  34.0 1.6 collective-permute-start.6
  35.6 1.1 collective-permute-start.4
  36.6 4.9 constant_dynamic-update-slice_fusion.1
  41.6 11.8 %collective-permute-done.4 = bf16[4,64,1280]{2,1,0:T(8,128)(2,1)S(1)} collective-permute-done((bf16[4,64,1280]{2,1,0:T(8,128)(2,1)}, bf16[4,64,1280]{2,1,0:T(8,128)(2,1)S(1)}, u32[]{:S(2)}, u32[]{:S(2)}) %collective-permute-start.4) | collective-permute-done | bytes 655392 | tf_op jit(solution)/shard_map/ppermute | solution.py:36
  53.4 4.6 collective-permute-start.20
  58.9 1.3 collective-permute-start.21
  60.4 30.4 %collective-permute-done.20 = bf16[128,3584]{1,0:T(8,128)(2,1)S(1)} collective-permute-done((bf16[128,3584]{1,0:T(8,128)(2,1)S(1)}, bf16[128,3584]{1,0:T(8,128)(2,1)S(1)}, u32[]{:S(2)}, u32[]{:S(2)}) %collective-permute-start.20) | collective-permute-done | bytes 917536 | tf_op jit(solution)/shard_map/ppermute | solution.py:44
  91.5 4.6 collective-permute-done.21
  96.2 1.3 collective-permute-start.22
  99.1 1.3 collective-permute-start.15
  101.1 20.2 %collective-permute-done.22 = bf16[128,3584]{1,0:T(8,128)(2,1)S(1)} collective-permute-done((bf16[128,3584]{1,0:T(8,128)(2,1)S(1)}, bf16[128,3584]{1,0:T(8,128)(2,1)S(1)}, u32[]{:S(2)}, u32[]{:S(2)}) %collective-permute-start.22) | collective-permute-done | bytes 917536 | tf_op jit(solution)/shard_map/ppermute | solution.py:45
  121.3 1.3 collective-permute-start.23
  123.8 54.5 %collective-permute-done.23 = bf16[128,3584]{1,0:T(8,128)(2,1)S(1)} collective-permute-done((bf16[128,3584]{1,0:T(8,128)(2,1)S(1)}, bf16[128,3584]{1,0:T(8,128)(2,1)S(1)}, u32[]{:S(2)}, u32[]{:S(2)}) %collective-permute-start.23) | collective-permute-done | bytes 917536 | tf_op jit(solution)/shard_map/ppermute | solution.py:45
  178.4 2.2 fusion.28
  180.6 1.5 collective-permute-start.26
  182.1 1.5 collective-permute-start.16
  183.8 3.6 select_bitcast_fusion
  187.4 36.3 %collective-permute-done.16 = bf16[256,3584]{0,1:T(8,128)(2,1)S(1)} collective-permute-done((bf16[256,3584]{0,1:T(8,128)(2,1)S(1)}, bf16[256,3584]{0,1:T(8,128)(2,1)S(1)}, u32[]{:S(2)}, u32[]{:S(2)}) %collective-permute-start.16) | collective-permute-done | bytes 1835040 | tf_op jit(solution)/shard_map/ppermute | solution.py:45
  223.7 1.5 select_bitcast_fusion.2
  225.2 10.7 %convert_reduce_fusion.1 = bf16[3584,640]{1,0:T(8,128)(2,1)} fusion(bf16[4,256,640]{2,1,0:T(8,128)(2,1)S(1)} %get-tuple-element.8, bf16[1,256,3584]{1,2,0:T(8,128)(2,1)} %select_bitcast_fusion, bf16[1,256,3584]{1,2,0:T(8,128)(2,1)S(1)} %select_bitcast_fusion.1, bf16[1,256,3584]{1,2,0:T(8,128)(2,1)} %select_bitcast_fusion.2, ...), kind=kOutput, calls=%fused_computation.1 | convolution fusion | flops 4724686848 | bytes 13238272 | tf_op jit(solution)/shard_map/gtf,gtd->gfd/dot_general | solution.py:101
  236.5 4.9 constant_dynamic-update-slice_fusion
  241.4 8.1 %fusion.29 = (bf16[256,3584]{1,0:T(8,128)(2,1)S(1)}, f32[256,3584]{1,0:T(8,128)}) fusion(bf16[3584,1280]{1,0:T(8,128)(2,1)} %constant_dynamic-update-slice_fusion, bf16[4,256,640]{2,1,0:T(8,128)(2,1)S(1)} %get-tuple-element.8, bf16[4,256,640]{2,1,0:T(8,128)(2,1)S(1)} %get-tuple-element.7), kind=kOutput, calls=%fused_computation.105 | convolution fusion | flops 2351038464 | bytes 17301504 | tf_op jit(solution)/shard_map/dot_general | solution.py:83
  249.6 4.2 collective-permute-start.7
  253.7 3.5 fusion.4
  257.3 12.9 %convert_reduce_fusion = f32[3584,640]{1,0:T(8,128)} fusion(bf16[4,256,640]{2,1,0:T(8,128)(2,1)S(1)} %get-tuple-element.7, bf16[1,256,3584]{1,2,0:T(8,128)(2,1)} %select_bitcast_fusion, bf16[1,256,3584]{1,2,0:T(8,128)(2,1)} %copy-done.12, bf16[1,256,3584]{1,2,0:T(8,128)(2,1)} %select_bitcast_fusion.2, bf16[1,256,3584]{1,2,0:T(8,128)(2,1)} %bitcast.133), kind=kOutput, calls=%fused_computation | convolution fusion | flops 4733861888 | bytes 17825792 | tf_op jit(solution)/shard_map/gtf,gtd->gfd/dot_general | solution.py:101
  270.2 18.3 %collective-permute-done.7 = bf16[256,3584]{1,0:T(8,128)(2,1)} collective-permute-done((bf16[256,3584]{1,0:T(8,128)(2,1)S(1)}, bf16[256,3584]{1,0:T(8,128)(2,1)}, u32[]{:S(2)}, u32[]{:S(2)}) %collective-permute-start.7) | collective-permute-done | bytes 1835040 | tf_op jit(solution)/shard_map/ppermute | solution.py:92
  288.5 3.3 add_convert_fusion.3
  291.8 5.8 %collective-permute-start.8 = (bf16[256,3584]{1,0:T(8,128)(2,1)}, bf16[256,3584]{1,0:T(8,128)(2,1)}, u32[]{:S(2)}, u32[]{:S(2)}) collective-permute-start(bf16[256,3584]{1,0:T(8,128)(2,1)} %add_convert_fusion.3), channel_id=1, source_target_pairs={{0,8},{4,12},{8,16},{12,20},{1,9},{5,13},{9,17},{13,21},{2,10},{6,... | collective-permute-start | bytes 5505032 | tf_op jit(solution)/shard_map/ppermute | solution.py:92
  297.5 5.8 %pad_maximum_fusion.1 = bf16[2,4,128,3584]{3,2,1,0:T(8,128)(2,1)} fusion(bf16[1,4,128,3584]{3,2,1,0:T(8,128)(2,1)} %bitcast.22, bf16[1,4,128,3584]{3,2,1,0:T(8,128)(2,1)S(1)} %get-tuple-element.3), kind=kLoop, calls=%fused_computation.4 | loop fusion | flops 3670016 | bytes 14680064 | tf_op jit(solution)/shard_map/stack | solution.py:110
  303.3 55.3 %collective-permute-done.19 = bf16[3584,640]{1,0:T(8,128)(2,1)} collective-permute-done((bf16[3584,640]{1,0:T(8,128)(2,1)}, bf16[3584,640]{1,0:T(8,128)(2,1)}, u32[]{:S(2)}, u32[]{:S(2)}) %collective-permute-start.19) | collective-permute-done | bytes 4587552 | tf_op jit(solution)/shard_map/ppermute | solution.py:104
  358.6 10.2 %subtract_convert_fusion = bf16[3584,640]{1,0:T(8,128)(2,1)} fusion(f32[3584,640]{1,0:T(8,128)} %convert_reduce_fusion, bf16[3584,640]{1,0:T(8,128)(2,1)} %collective-permute-done.19, bf16[3584,640]{1,0:T(8,128)(2,1)} %param.6), kind=kLoop, calls=%fused_computation.2 | loop fusion | flops 13762560 | bytes 22937600 | tf_op jit(solution)/shard_map/convert_element_type | solution.py:106
  368.8 9.6 %convolution_convert_fusion = bf16[1024,640]{1,0:T(8,128)(2,1)S(1)} fusion(bf16[1024,3584]{1,0:T(8,128)(2,1)} %bitcast.129, bf16[3584,640]{1,0:T(8,128)(2,1)} %subtract_convert_fusion), kind=kOutput, calls=%fused_computation.23 | convolution fusion | flops 4698275840 | bytes 13238272 | tf_op jit(solution)/shard_map/dot_general | solution.py:111
  378.6 2.6 collective-permute-start.28
  381.3 8.5 %add_convert_fusion.2 = (bf16[256,3584]{1,0:T(8,128)(2,1)}, bf16[256,3584]{1,0:T(8,128)(2,1)}) fusion(bf16[256,3584]{1,0:T(8,128)(2,1)} %collective-permute-done.8, bf16[3584,1280]{1,0:T(8,128)(2,1)} %constant_dynamic-update-slice_fusion, bf16[4,256,640]{2,1,0:T(8,128)(2,1)S(1)} %copy-done.6, bf16[4,256,640]{2,1,0:T(8,128)(2,1)S(1)} %copy-done.9), kind=kOutput, calls=%fused_computation.11 | convolution fusion | flops 2353790976 | bytes 17301504 | tf_op jit(solution)/shard_map/dot_general | solution.py:83
  390.6 2.7 collective-permute-start.9
  393.3 3.2 collective-permute-done.28
  396.7 1.4 collective-permute-start.30
  398.1 1.1 collective-permute-start.31
  399.2 1.9 collective-permute-start.32
  401.2 32.4 %collective-permute-done.30 = bf16[32,640]{1,0:T(8,128)(2,1)S(1)} collective-permute-done((bf16[32,640]{1,0:T(8,128)(2,1)S(1)}, bf16[32,640]{1,0:T(8,128)(2,1)S(1)}, u32[]{:S(2)}, u32[]{:S(2)}) %collective-permute-start.30) | collective-permute-done | bytes 40992 | tf_op jit(solution)/shard_map/ppermute | solution.py:129
  433.5 1.5 collective-permute-start.33
  435.0 7.8 %collective-permute-start.34 = (bf16[32,640]{1,0:T(8,128)(2,1)S(1)}, bf16[32,640]{1,0:T(8,128)(2,1)S(1)}, u32[]{:S(2)}, u32[]{:S(2)}) collective-permute-start(bf16[32,640]{1,0:T(8,128)(2,1)S(1)} %get-tuple-element.18), channel_id=1, source_target_pairs={{0,28},{4,24},{8,4},{12,0},{16,12},{20,8},{24,20},{28,16},{1,29},{... | collective-permute-start | bytes 122888 | tf_op jit(solution)/shard_map/ppermute | solution.py:129
  444.5 4.2 collective-permute-done.35
  448.7 1.0 collective-permute-done.36
  450.1 1.7 rev.3
  453.1 1.0 reshape.53
  454.0 3.7 add_convert_fusion.1
  459.5 10.0 %collective-permute-done.38 = bf16[32,5120]{1,0:T(8,128)(2,1)} collective-permute-done((bf16[32,5120]{1,0:T(8,128)(2,1)}, bf16[32,5120]{1,0:T(8,128)(2,1)}, u32[]{:S(2)}, u32[]{:S(2)}) %collective-permute-start.38) | collective-permute-done | bytes 327712 | tf_op jit(solution)/shard_map/ppermute | solution.py:36
  469.4 1.0 bitcast_dynamic-update-slice_fusion.10
  470.4 2.0 collective-permute-done.39
  472.5 1.0 bitcast_dynamic-update-slice_fusion.11
  474.0 1.4 collective-permute-start.12
  475.5 1.2 constant_dynamic-slice_fusion
  476.6 68.1 %collective-permute-done.12 = bf16[256,3584]{1,0:T(8,128)(2,1)S(1)} collective-permute-done((bf16[256,3584]{1,0:T(8,128)(2,1)S(1)}, bf16[256,3584]{1,0:T(8,128)(2,1)S(1)}, u32[]{:S(2)}, u32[]{:S(2)}) %collective-permute-start.12) | collective-permute-done | bytes 1835040 | tf_op jit(solution)/shard_map/ppermute | solution.py:93
  544.7 8.2 %fusion.1 = bf16[256,3584]{1,0:T(8,128)(2,1)} fusion(bf16[3584,1280]{1,0:T(8,128)(2,1)} %constant_dynamic-update-slice_fusion, bf16[256,3584]{1,0:T(8,128)(2,1)S(1)} %collective-permute-done.12, bf16[256,3584]{1,0:T(8,128)(2,1)} %collective-permute-done.9, bf16[4,256,640]{2,1,0:T(8,128)(2,1)S(1)} %copy-done.7, bf16[4,256,640]{2,1,0:T(8,128)(2,1)S(1)} %copy-done.10), kind=kOutput, calls=%fused_computation.7 | convolution fusion | flops 2354708480 | bytes 17301504 | tf_op jit(solution)/shard_map/dot_general | solution.py:83
  (113 shorter events, 15.2 us)
Async XLA Ops:
  0.6 1.7 copy-start
  4.3 9.8 %collective-permute-start.2 = (bf16[64,1280]{1,0:T(8,128)(2,1)S(1)}, bf16[64,1280]{1,0:T(8,128)(2,1)S(1)}, u32[]{:S(2)}, u32[]{:S(2)}) collective-permute-start(bf16[64,1280]{1,0:T(8,128)(2,1)S(1)} %bitcast.152), channel_id=1, source_target_pairs={{0,24},{4,28},{8,0},{12,4},{16,8},{20,12},{24,16},{28,20},{1,25},{... | collective-permute-start | bytes 491528 | tf_op jit(solution)/shard_map/ppermute | solution.py:22
  9.4 13.9 %collective-permute-start.1 = (bf16[64,1280]{1,0:T(8,128)(2,1)S(1)}, bf16[64,1280]{1,0:T(8,128)(2,1)S(1)}, u32[]{:S(2)}, u32[]{:S(2)}) collective-permute-start(bf16[64,1280]{1,0:T(8,128)(2,1)S(1)} %bitcast.153), channel_id=1, source_target_pairs={{0,16},{4,20},{8,24},{12,28},{16,0},{20,4},{24,8},{28,12},{1,17},{... | collective-permute-start | bytes 491528 | tf_op jit(solution)/shard_map/ppermute | solution.py:22
  9.6 13.8 %collective-permute-start = (bf16[64,1280]{1,0:T(8,128)(2,1)S(1)}, bf16[64,1280]{1,0:T(8,128)(2,1)S(1)}, u32[]{:S(2)}, u32[]{:S(2)}) collective-permute-start(bf16[64,1280]{1,0:T(8,128)(2,1)S(1)} %bitcast.154), channel_id=1, source_target_pairs={{0,8},{4,12},{8,16},{12,20},{16,24},{20,28},{24,0},{28,4},{1,9},{5... | collective-permute-start | bytes 491528 | tf_op jit(solution)/shard_map/ppermute | solution.py:22
  24.2 17.3 %collective-permute-start.3 = (bf16[4,64,1280]{2,1,0:T(8,128)(2,1)}, bf16[4,64,1280]{2,1,0:T(8,128)(2,1)S(1)}, u32[]{:S(2)}, u32[]{:S(2)}) collective-permute-start(bf16[4,64,1280]{2,1,0:T(8,128)(2,1)} %pad_maximum_fusion.6), channel_id=1, source_target_pairs={{0,3},{1,0},{2,1},{3,2},{4,7},{5,4},{6,5},{7,6},{8,11},{9,8},{10,9... | collective-permute-start | bytes 1966088 | tf_op jit(solution)/shard_map/ppermute | solution.py:36
  28.7 24.8 %copy-start.13 = (bf16[128,3584]{1,0:T(8,128)(2,1)S(1)}, bf16[128,3584]{1,0:T(8,128)(2,1)}, u32[]{:S(2)}) copy-start(bf16[128,3584]{1,0:T(8,128)(2,1)} %param.7) | copy-start | bytes 2752516
  28.7 69.6 %collective-permute-start.13 = (bf16[256,3584]{0,1:T(8,128)(2,1)}, bf16[256,3584]{0,1:T(8,128)(2,1)}, u32[]{:S(2)}, u32[]{:S(2)}) collective-permute-start(bf16[256,3584]{0,1:T(8,128)(2,1)} %copy.24), channel_id=1, source_target_pairs={{0,8},{4,12},{8,16},{12,20},{16,24},{20,28},{1,9},{5,13},{9,17},{1... | collective-permute-start | bytes 5505032 | tf_op jit(solution)/shard_map/ppermute | solution.py:44
  32.7 66.4 %collective-permute-start.14 = (bf16[256,3584]{0,1:T(8,128)(2,1)}, bf16[256,3584]{0,1:T(8,128)(2,1)}, u32[]{:S(2)}, u32[]{:S(2)}) collective-permute-start(bf16[256,3584]{0,1:T(8,128)(2,1)} %copy.24), channel_id=1, source_target_pairs={{8,0},{12,4},{16,8},{20,12},{24,16},{28,20},{9,1},{13,5},{17,9},{2... | collective-permute-start | bytes 5505032 | tf_op jit(solution)/shard_map/ppermute | solution.py:45
  34.0 202.5 %collective-permute-start.6 = (bf16[3584,640]{1,0:T(8,128)(2,1)}, bf16[3584,640]{1,0:T(8,128)(2,1)}, u32[]{:S(2)}, u32[]{:S(2)}) collective-permute-start(bf16[3584,640]{1,0:T(8,128)(2,1)} %param.6), channel_id=1, source_target_pairs={{0,4},{4,0},{8,12},{12,8},{16,20},{20,16},{24,28},{28,24},{1,5},{5... | collective-permute-start | bytes 13762568 | tf_op jit(solution)/shard_map/ppermute | solution.py:77
  35.6 17.9 %collective-permute-start.4 = (bf16[4,64,1280]{2,1,0:T(8,128)(2,1)}, bf16[4,64,1280]{2,1,0:T(8,128)(2,1)S(1)}, u32[]{:S(2)}, u32[]{:S(2)}) collective-permute-start(bf16[4,64,1280]{2,1,0:T(8,128)(2,1)} %pad_maximum_fusion.6), channel_id=1, source_target_pairs={{0,2},{1,3},{2,0},{3,1},{4,6},{5,7},{6,4},{7,5},{8,10},{9,11},{10,... | collective-permute-start | bytes 1966088 | tf_op jit(solution)/shard_map/ppermute | solution.py:36
  41.5 17.4 %collective-permute-start.5 = (bf16[4,64,1280]{2,1,0:T(8,128)(2,1)}, bf16[4,64,1280]{2,1,0:T(8,128)(2,1)S(1)}, u32[]{:S(2)}, u32[]{:S(2)}) collective-permute-start(bf16[4,64,1280]{2,1,0:T(8,128)(2,1)} %pad_maximum_fusion.6), channel_id=1, source_target_pairs={{0,1},{1,2},{2,3},{3,0},{4,5},{5,6},{6,7},{7,4},{8,9},{9,10},{10,1... | collective-permute-start | bytes 1966088 | tf_op jit(solution)/shard_map/ppermute | solution.py:36
  53.4 37.4 %collective-permute-start.20 = (bf16[128,3584]{1,0:T(8,128)(2,1)S(1)}, bf16[128,3584]{1,0:T(8,128)(2,1)S(1)}, u32[]{:S(2)}, u32[]{:S(2)}) collective-permute-start(bf16[128,3584]{1,0:T(8,128)(2,1)S(1)} %copy-done.13), channel_id=1, source_target_pairs={{0,8},{4,12},{8,16},{12,20},{16,24},{20,28},{1,9},{5,13},{9,17},{1... | collective-permute-start | bytes 2752520 | tf_op jit(solution)/shard_map/ppermute | solution.py:44
  58.9 37.2 %collective-permute-start.21 = (bf16[128,3584]{1,0:T(8,128)(2,1)S(1)}, bf16[128,3584]{1,0:T(8,128)(2,1)S(1)}, u32[]{:S(2)}, u32[]{:S(2)}) collective-permute-start(bf16[128,3584]{1,0:T(8,128)(2,1)S(1)} %copy-done.13), channel_id=1, source_target_pairs={{8,0},{12,4},{16,8},{20,12},{24,16},{28,20},{9,1},{13,5},{17,9},{2... | collective-permute-start | bytes 2752520 | tf_op jit(solution)/shard_map/ppermute | solution.py:45
  90.8 9.6 %collective-permute-start.24 = (bf16[128,3584]{1,0:T(8,128)(2,1)S(1)}, bf16[128,3584]{1,0:T(8,128)(2,1)S(1)}, u32[]{:S(2)}, u32[]{:S(2)}) collective-permute-start(bf16[128,3584]{1,0:T(8,128)(2,1)S(1)} %collective-permute-done.20), channel_id=1, source_target_pairs={{8,16},{12,20},{16,24},{20,28},{9,17},{13,21},{17,25},{21,29},{10,... | collective-permute-start | bytes 2752520 | tf_op jit(solution)/shard_map/ppermute | solution.py:44
  96.2 25.2 %collective-permute-start.22 = (bf16[128,3584]{1,0:T(8,128)(2,1)S(1)}, bf16[128,3584]{1,0:T(8,128)(2,1)S(1)}, u32[]{:S(2)}, u32[]{:S(2)}) collective-permute-start(bf16[128,3584]{1,0:T(8,128)(2,1)S(1)} %collective-permute-done.21), channel_id=1, source_target_pairs={{8,0},{12,4},{16,8},{20,12},{9,1},{13,5},{17,9},{21,13},{10,2},{14... | collective-permute-start | bytes 2752520 | tf_op jit(solution)/shard_map/ppermute | solution.py:45
  98.3 143.2 %copy-start.8 = (bf16[4,256,640]{2,1,0:T(8,128)(2,1)}, bf16[4,256,640]{2,1,0:T(8,128)(2,1)S(1)}, u32[]{:S(2)}) copy-start(bf16[4,256,640]{2,1,0:T(8,128)(2,1)S(1)} %get-tuple-element.8) | copy-start | bytes 3932164
  98.3 159.0 %copy-start.5 = (bf16[4,256,640]{2,1,0:T(8,128)(2,1)}, bf16[4,256,640]{2,1,0:T(8,128)(2,1)S(1)}, u32[]{:S(2)}) copy-start(bf16[4,256,640]{2,1,0:T(8,128)(2,1)S(1)} %get-tuple-element.7) | copy-start | bytes 3932164
  98.3 24.6 %collective-permute-start.17 = (bf16[256,3584]{0,1:T(8,128)(2,1)}, bf16[256,3584]{0,1:T(8,128)(2,1)S(1)}, u32[]{:S(2)}, u32[]{:S(2)}) collective-permute-start(bf16[256,3584]{0,1:T(8,128)(2,1)} %collective-permute-done.13), channel_id=1, source_target_pairs={{8,16},{12,20},{16,24},{20,28},{9,17},{13,21},{17,25},{21,29},{10,... | collective-permute-start | bytes 5505032 | tf_op jit(solution)/shard_map/ppermute | solution.py:44
  99.1 83.0 %collective-permute-start.15 = (bf16[256,3584]{0,1:T(8,128)(2,1)}, bf16[256,3584]{0,1:T(8,128)(2,1)S(1)}, u32[]{:S(2)}, u32[]{:S(2)}) collective-permute-start(bf16[256,3584]{0,1:T(8,128)(2,1)} %collective-permute-done.14), channel_id=1, source_target_pairs={{8,0},{12,4},{16,8},{20,12},{9,1},{13,5},{17,9},{21,13},{10,2},{14... | collective-permute-start | bytes 5505032 | tf_op jit(solution)/shard_map/ppermute | solution.py:45
  100.4 22.4 %collective-permute-start.25 = (bf16[128,3584]{1,0:T(8,128)(2,1)S(1)}, bf16[128,3584]{1,0:T(8,128)(2,1)S(1)}, u32[]{:S(2)}, u32[]{:S(2)}) collective-permute-start(bf16[128,3584]{1,0:T(8,128)(2,1)S(1)} %collective-permute-done.24), channel_id=1, source_target_pairs={{16,24},{20,28},{17,25},{21,29},{18,26},{22,30},{19,27},{23,31}} | collective-permute-start | bytes 2752520 | tf_op jit(solution)/shard_map/ppermute | solution.py:44
  121.3 57.0 %collective-permute-start.23 = (bf16[128,3584]{1,0:T(8,128)(2,1)S(1)}, bf16[128,3584]{1,0:T(8,128)(2,1)S(1)}, u32[]{:S(2)}, u32[]{:S(2)}) collective-permute-start(bf16[128,3584]{1,0:T(8,128)(2,1)S(1)} %collective-permute-done.22), channel_id=1, source_target_pairs={{8,0},{12,4},{9,1},{13,5},{10,2},{14,6},{11,3},{15,7}} | collective-permute-start | bytes 2752520 | tf_op jit(solution)/shard_map/ppermute | solution.py:45
  122.7 55.7 %copy-start.14 = (bf16[128,3584]{1,0:T(8,128)(2,1)S(1)}, bf16[128,3584]{1,0:T(8,128)(2,1)}, u32[]{:S(2)}) copy-start(bf16[128,3584]{1,0:T(8,128)(2,1)} %param.7) | copy-start | bytes 2752516
  122.9 60.9 %collective-permute-start.18 = (bf16[256,3584]{0,1:T(8,128)(2,1)S(1)}, bf16[256,3584]{0,1:T(8,128)(2,1)S(1)}, u32[]{:S(2)}, u32[]{:S(2)}) collective-permute-start(bf16[256,3584]{0,1:T(8,128)(2,1)S(1)} %collective-permute-done.17), channel_id=1, source_target_pairs={{16,24},{20,28},{17,25},{21,29},{18,26},{22,30},{19,27},{23,31}} | collective-permute-start | bytes 5505032 | tf_op jit(solution)/shard_map/ppermute | solution.py:44
  180.6 116.9 %collective-permute-start.26 = (bf16[4,128,3584]{2,1,0:T(8,128)(2,1)}, bf16[4,128,3584]{2,1,0:T(8,128)(2,1)}, u32[]{:S(2)}, u32[]{:S(2)}) collective-permute-start(bf16[4,128,3584]{2,1,0:T(8,128)(2,1)} %get-tuple-element.4), channel_id=1, source_target_pairs={{0,4},{4,0},{8,12},{12,8},{16,20},{20,16},{24,28},{28,24},{1,5},{5... | collective-permute-start | bytes 11010056 | tf_op jit(solution)/shard_map/ppermute | solution.py:109
  182.1 41.6 %collective-permute-start.16 = (bf16[256,3584]{0,1:T(8,128)(2,1)S(1)}, bf16[256,3584]{0,1:T(8,128)(2,1)S(1)}, u32[]{:S(2)}, u32[]{:S(2)}) collective-permute-start(bf16[256,3584]{0,1:T(8,128)(2,1)S(1)} %collective-permute-done.15), channel_id=1, source_target_pairs={{8,0},{12,4},{9,1},{13,5},{10,2},{14,6},{11,3},{15,7}} | collective-permute-start | bytes 5505032 | tf_op jit(solution)/shard_map/ppermute | solution.py:45
  183.8 41.5 %copy-start.12 = (bf16[1,256,3584]{1,2,0:T(8,128)(2,1)}, bf16[1,256,3584]{1,2,0:T(8,128)(2,1)S(1)}, u32[]{:S(2)}) copy-start(bf16[1,256,3584]{1,2,0:T(8,128)(2,1)S(1)} %select_bitcast_fusion.1) | copy-start | bytes 5505028
  187.4 37.9 %copy-start.11 = (bf16[256,3584]{0,1:T(8,128)(2,1)S(1)}, bf16[256,3584]{0,1:T(8,128)(2,1)}, u32[]{:S(2)}) copy-start(bf16[256,3584]{0,1:T(8,128)(2,1)} %copy.24) | copy-start | bytes 5505028
  236.0 122.6 %collective-permute-start.19 = (bf16[3584,640]{1,0:T(8,128)(2,1)}, bf16[3584,640]{1,0:T(8,128)(2,1)}, u32[]{:S(2)}, u32[]{:S(2)}) collective-permute-start(bf16[3584,640]{1,0:T(8,128)(2,1)} %convert_reduce_fusion.1), channel_id=1, source_target_pairs={{0,4},{4,0},{8,12},{12,8},{16,20},{20,16},{24,28},{28,24},{1,5},{5... | collective-permute-start | bytes 13762568 | tf_op jit(solution)/shard_map/ppermute | solution.py:104
  241.4 12.3 %copy-start.2 = (bf16[3584,1280]{1,0:T(8,128)(2,1)S(1)}, bf16[3584,1280]{1,0:T(8,128)(2,1)}, u32[]{:S(2)}) copy-start(bf16[3584,1280]{1,0:T(8,128)(2,1)} %constant_dynamic-update-slice_fusion) | copy-start | bytes 27525124
  249.6 39.0 %collective-permute-start.7 = (bf16[256,3584]{1,0:T(8,128)(2,1)S(1)}, bf16[256,3584]{1,0:T(8,128)(2,1)}, u32[]{:S(2)}, u32[]{:S(2)}) collective-permute-start(bf16[256,3584]{1,0:T(8,128)(2,1)S(1)} %get-tuple-element.23), channel_id=1, source_target_pairs={{0,8},{4,12},{1,9},{5,13},{2,10},{6,14},{3,11},{7,15}} | collective-permute-start | bytes 5505032 | tf_op jit(solution)/shard_map/ppermute | solution.py:92
  257.3 31.2 %copy-start.4 = (f32[256,3584]{1,0:T(8,128)}, f32[256,3584]{1,0:T(8,128)S(1)}, u32[]{:S(2)}) copy-start(f32[256,3584]{1,0:T(8,128)S(1)} %fusion.4) | copy-start | bytes 11010052
  291.8 89.6 %collective-permute-start.8 = (bf16[256,3584]{1,0:T(8,128)(2,1)}, bf16[256,3584]{1,0:T(8,128)(2,1)}, u32[]{:S(2)}, u32[]{:S(2)}) collective-permute-start(bf16[256,3584]{1,0:T(8,128)(2,1)} %add_convert_fusion.3), channel_id=1, source_target_pairs={{0,8},{4,12},{8,16},{12,20},{1,9},{5,13},{9,17},{13,21},{2,10},{6,... | collective-permute-start | bytes 5505032 | tf_op jit(solution)/shard_map/ppermute | solution.py:92
  368.8 12.6 %copy-start.6 = (bf16[4,256,640]{2,1,0:T(8,128)(2,1)S(1)}, bf16[4,256,640]{2,1,0:T(8,128)(2,1)}, u32[]{:S(2)}) copy-start(bf16[4,256,640]{2,1,0:T(8,128)(2,1)} %copy-done.5) | copy-start | bytes 3932164
  368.8 12.6 %copy-start.9 = (bf16[4,256,640]{2,1,0:T(8,128)(2,1)S(1)}, bf16[4,256,640]{2,1,0:T(8,128)(2,1)}, u32[]{:S(2)}) copy-start(bf16[4,256,640]{2,1,0:T(8,128)(2,1)} %copy-done.8) | copy-start | bytes 3932164
  378.5 14.8 %collective-permute-start.29 = (bf16[8,32,640]{2,1,0:T(8,128)(2,1)S(1)}, bf16[8,32,640]{2,1,0:T(8,128)(2,1)S(1)}, u32[]{:S(2)}, u32[]{:S(2)}) collective-permute-start(bf16[8,32,640]{2,1,0:T(8,128)(2,1)S(1)} %get-tuple-element.10), channel_id=1, source_target_pairs={{0,3},{1,0},{2,1},{3,2},{4,7},{5,4},{6,5},{7,6},{8,11},{9,8},{10,9... | collective-permute-start | bytes 983048 | tf_op jit(solution)/shard_map/ppermute | solution.py:22
  378.6 17.9 %collective-permute-start.28 = (bf16[8,32,640]{2,1,0:T(8,128)(2,1)S(1)}, bf16[8,32,640]{2,1,0:T(8,128)(2,1)S(1)}, u32[]{:S(2)}, u32[]{:S(2)}) collective-permute-start(bf16[8,32,640]{2,1,0:T(8,128)(2,1)S(1)} %get-tuple-element.11), channel_id=1, source_target_pairs={{0,2},{1,3},{2,0},{3,1},{4,6},{5,7},{6,4},{7,5},{8,10},{9,11},{10,... | collective-permute-start | bytes 983048 | tf_op jit(solution)/shard_map/ppermute | solution.py:22
  381.2 15.3 %collective-permute-start.27 = (bf16[8,32,640]{2,1,0:T(8,128)(2,1)S(1)}, bf16[8,32,640]{2,1,0:T(8,128)(2,1)S(1)}, u32[]{:S(2)}, u32[]{:S(2)}) collective-permute-start(bf16[8,32,640]{2,1,0:T(8,128)(2,1)S(1)} %get-tuple-element.9), channel_id=1, source_target_pairs={{0,1},{1,2},{2,3},{3,0},{4,5},{5,6},{6,7},{7,4},{8,9},{9,10},{10,1... | collective-permute-start | bytes 983048 | tf_op jit(solution)/shard_map/ppermute | solution.py:22
  389.9 64.2 %collective-permute-start.10 = (bf16[256,3584]{1,0:T(8,128)(2,1)}, bf16[256,3584]{1,0:T(8,128)(2,1)S(1)}, u32[]{:S(2)}, u32[]{:S(2)}) collective-permute-start(bf16[256,3584]{1,0:T(8,128)(2,1)} %get-tuple-element.6), channel_id=1, source_target_pairs={{24,16},{28,20},{25,17},{29,21},{26,18},{30,22},{27,19},{31,23}} | collective-permute-start | bytes 5505032 | tf_op jit(solution)/shard_map/ppermute | solution.py:93
  390.6 86.0 %collective-permute-start.9 = (bf16[256,3584]{1,0:T(8,128)(2,1)}, bf16[256,3584]{1,0:T(8,128)(2,1)}, u32[]{:S(2)}, u32[]{:S(2)}) collective-permute-start(bf16[256,3584]{1,0:T(8,128)(2,1)} %get-tuple-element.5), channel_id=1, source_target_pairs={{0,8},{4,12},{8,16},{12,20},{16,24},{20,28},{1,9},{5,13},{9,17},{1... | collective-permute-start | bytes 5505032 | tf_op jit(solution)/shard_map/ppermute | solution.py:92
  396.7 36.8 %collective-permute-start.30 = (bf16[32,640]{1,0:T(8,128)(2,1)S(1)}, bf16[32,640]{1,0:T(8,128)(2,1)S(1)}, u32[]{:S(2)}, u32[]{:S(2)}) collective-permute-start(bf16[32,640]{1,0:T(8,128)(2,1)S(1)} %get-tuple-element.22), channel_id=1, source_target_pairs={{0,24},{4,28},{8,0},{12,4},{16,8},{20,12},{24,16},{28,20},{1,25},{... | collective-permute-start | bytes 122888 | tf_op jit(solution)/shard_map/ppermute | solution.py:129
  398.1 36.9 %collective-permute-start.31 = (bf16[32,640]{1,0:T(8,128)(2,1)S(1)}, bf16[32,640]{1,0:T(8,128)(2,1)S(1)}, u32[]{:S(2)}, u32[]{:S(2)}) collective-permute-start(bf16[32,640]{1,0:T(8,128)(2,1)S(1)} %get-tuple-element.21), channel_id=1, source_target_pairs={{0,16},{4,20},{8,24},{12,28},{16,0},{20,4},{24,8},{28,12},{1,17},{... | collective-permute-start | bytes 122888 | tf_op jit(solution)/shard_map/ppermute | solution.py:129
  399.2 43.6 %collective-permute-start.32 = (bf16[32,640]{1,0:T(8,128)(2,1)S(1)}, bf16[32,640]{1,0:T(8,128)(2,1)S(1)}, u32[]{:S(2)}, u32[]{:S(2)}) collective-permute-start(bf16[32,640]{1,0:T(8,128)(2,1)S(1)} %get-tuple-element.20), channel_id=1, source_target_pairs={{0,8},{4,12},{8,16},{12,20},{16,24},{20,28},{24,0},{28,4},{1,9},{5... | collective-permute-start | bytes 122888 | tf_op jit(solution)/shard_map/ppermute | solution.py:129
  433.5 9.4 %collective-permute-start.33 = (bf16[32,640]{1,0:T(8,128)(2,1)S(1)}, bf16[32,640]{1,0:T(8,128)(2,1)S(1)}, u32[]{:S(2)}, u32[]{:S(2)}) collective-permute-start(bf16[32,640]{1,0:T(8,128)(2,1)S(1)} %get-tuple-element.19), channel_id=1, source_target_pairs={{0,4},{4,0},{8,12},{12,8},{16,20},{20,16},{24,28},{28,24},{1,5},{5... | collective-permute-start | bytes 122888 | tf_op jit(solution)/shard_map/ppermute | solution.py:129
  435.0 9.5 %collective-permute-start.34 = (bf16[32,640]{1,0:T(8,128)(2,1)S(1)}, bf16[32,640]{1,0:T(8,128)(2,1)S(1)}, u32[]{:S(2)}, u32[]{:S(2)}) collective-permute-start(bf16[32,640]{1,0:T(8,128)(2,1)S(1)} %get-tuple-element.18), channel_id=1, source_target_pairs={{0,28},{4,24},{8,4},{12,0},{16,12},{20,8},{24,20},{28,16},{1,29},{... | collective-permute-start | bytes 122888 | tf_op jit(solution)/shard_map/ppermute | solution.py:129
  442.8 5.9 %collective-permute-start.35 = (bf16[32,640]{1,0:T(8,128)(2,1)S(1)}, bf16[32,640]{1,0:T(8,128)(2,1)S(1)}, u32[]{:S(2)}, u32[]{:S(2)}) collective-permute-start(bf16[32,640]{1,0:T(8,128)(2,1)S(1)} %get-tuple-element.17), channel_id=1, source_target_pairs={{0,20},{4,16},{8,28},{12,24},{16,4},{20,0},{24,12},{28,8},{1,21},{... | collective-permute-start | bytes 122888 | tf_op jit(solution)/shard_map/ppermute | solution.py:129
  442.9 6.8 %collective-permute-start.36 = (bf16[32,640]{1,0:T(8,128)(2,1)S(1)}, bf16[32,640]{1,0:T(8,128)(2,1)S(1)}, u32[]{:S(2)}, u32[]{:S(2)}) collective-permute-start(bf16[32,640]{1,0:T(8,128)(2,1)S(1)} %get-tuple-element.16), channel_id=1, source_target_pairs={{0,12},{4,8},{8,20},{12,16},{16,28},{20,24},{24,4},{28,0},{1,13},{... | collective-permute-start | bytes 122888 | tf_op jit(solution)/shard_map/ppermute | solution.py:129
  454.0 5.4 collective-permute-start.37
  457.8 15.8 %collective-permute-start.11 = (bf16[256,3584]{1,0:T(8,128)(2,1)}, bf16[256,3584]{1,0:T(8,128)(2,1)S(1)}, u32[]{:S(2)}, u32[]{:S(2)}) collective-permute-start(bf16[256,3584]{1,0:T(8,128)(2,1)} %add_convert_fusion.1), channel_id=1, source_target_pairs={{16,8},{20,12},{24,16},{28,20},{17,9},{21,13},{25,17},{29,21},{18,... | collective-permute-start | bytes 5505032 | tf_op jit(solution)/shard_map/ppermute | solution.py:93
  458.5 10.9 %collective-permute-start.38 = (bf16[32,5120]{1,0:T(8,128)(2,1)}, bf16[32,5120]{1,0:T(8,128)(2,1)}, u32[]{:S(2)}, u32[]{:S(2)}) collective-permute-start(bf16[32,5120]{1,0:T(8,128)(2,1)} %reshape.53), channel_id=1, source_target_pairs={{0,2},{1,3},{2,0},{3,1},{4,6},{5,7},{6,4},{7,5},{8,10},{9,11},{10,... | collective-permute-start | bytes 983048 | tf_op jit(solution)/shard_map/ppermute | solution.py:36
  458.6 13.8 %collective-permute-start.39 = (bf16[32,5120]{1,0:T(8,128)(2,1)}, bf16[32,5120]{1,0:T(8,128)(2,1)S(1)}, u32[]{:S(2)}, u32[]{:S(2)}) collective-permute-start(bf16[32,5120]{1,0:T(8,128)(2,1)} %reshape.53), channel_id=1, source_target_pairs={{0,1},{1,2},{2,3},{3,0},{4,5},{5,6},{6,7},{7,4},{8,9},{9,10},{10,1... | collective-permute-start | bytes 983048 | tf_op jit(solution)/shard_map/ppermute | solution.py:36
  459.4 14.1 %copy-start.3 = (f32[256,3584]{1,0:T(8,128)S(1)}, f32[256,3584]{1,0:T(8,128)}, u32[]{:S(2)}) copy-start(f32[256,3584]{1,0:T(8,128)} %get-tuple-element.24) | copy-start | bytes 11010052
  474.0 70.8 %copy-start.7 = (bf16[4,256,640]{2,1,0:T(8,128)(2,1)S(1)}, bf16[4,256,640]{2,1,0:T(8,128)(2,1)}, u32[]{:S(2)}) copy-start(bf16[4,256,640]{2,1,0:T(8,128)(2,1)} %copy-done.5) | copy-start | bytes 3932164
  474.0 70.8 %copy-start.10 = (bf16[4,256,640]{2,1,0:T(8,128)(2,1)S(1)}, bf16[4,256,640]{2,1,0:T(8,128)(2,1)}, u32[]{:S(2)}) copy-start(bf16[4,256,640]{2,1,0:T(8,128)(2,1)} %copy-done.8) | copy-start | bytes 3932164
  474.0 70.7 %collective-permute-start.12 = (bf16[256,3584]{1,0:T(8,128)(2,1)S(1)}, bf16[256,3584]{1,0:T(8,128)(2,1)S(1)}, u32[]{:S(2)}, u32[]{:S(2)}) collective-permute-start(bf16[256,3584]{1,0:T(8,128)(2,1)S(1)} %add_convert_fusion), channel_id=1, source_target_pairs={{8,0},{12,4},{16,8},{20,12},{24,16},{28,20},{9,1},{13,5},{17,9},{2... | collective-permute-start | bytes 5505032 | tf_op jit(solution)/shard_map/ppermute | solution.py:93
  544.7 8.2 %copy-start.1 = (bf16[256,5120]{1,0:T(8,128)(2,1)S(1)}, bf16[256,5120]{1,0:T(8,128)(2,1)}, u32[]{:S(2)}) copy-start(bf16[256,5120]{1,0:T(8,128)(2,1)} %param.5) | copy-start | bytes 7864324

commit v2 on v1

--- a/solution.py
+++ b/solution.py
@@ -1,8 +1,11 @@
+import functools
 import math
 
 import jax
 import jax.numpy as jnp
 from jax import lax
+from jax.experimental import pallas as pl
+from jax.experimental.pallas import tpu as pltpu
 from jax.sharding import PartitionSpec as P
 
 F32, BF16 = jnp.float32, jnp.bfloat16
@@ -46,6 +49,130 @@
     return [block] + [
         jnp.where(at >= k, up[k], down[length - k]) for k in range(1, length)
     ]
+
+
+def opening_kernel(n_fsdp, n_tp, hidden, weight, cot, hid, peer, cots,
+                   up_send, down_send, hid_recv, w_send, w_recv,
+                   line_send, line_recv, tp_send, tp_recv, own):
+    length = n_fsdp // 2
+    me, tp = lax.axis_index("fsdp"), lax.axis_index("tp")
+    z, x = me // 2, me % 2
+    part = cot.shape[0] // n_tp
+    wide = 2 * weight.shape[1]
+
+    def at_line(index):
+        return {"fsdp": 2 * index + x}
+
+    def at_tp(k):
+        return {"tp": lax.rem(tp + k, n_tp)}
+
+    pair = {"fsdp": 2 * z + 1 - x}
+
+    def remote(src, dst, send, recv, device):
+        return pltpu.make_async_remote_copy(
+            src_ref=src, dst_ref=dst, send_sem=send, recv_sem=recv,
+            device_id=device, device_id_type=pl.DeviceIdType.MESH,
+        )
+
+    barrier = pltpu.get_barrier_semaphore()
+    partners = [pair] + [at_line(lax.rem(z + k, length)) for k in range(1, length)]
+    partners += [at_tp(k) for k in range(1, n_tp)]
+    for device in partners:
+        pl.semaphore_signal(
+            barrier, inc=1, device_id=device, device_id_type=pl.DeviceIdType.MESH
+        )
+    pl.semaphore_wait(barrier, len(partners))
+
+    def to_up(source, slot):
+        return remote(source, hid.at[slot], up_send.at[slot], hid_recv.at[slot], at_line(z + 1))
+
+    def to_down(source, slot):
+        return remote(source, hid.at[slot], down_send.at[slot], hid_recv.at[slot], at_line(z - 1))
+
+    rows = pl.ds(pl.multiple_of(tp * part, part), part)
+
+    def to_line(k):
+        other = lax.rem(z + k, length)
+        columns = pl.ds(pl.multiple_of(other * wide, wide), wide)
+        return remote(
+            cot.at[rows, columns], cots.at[tp, z], line_send.at[k], line_recv.at[k],
+            at_line(other),
+        )
+
+    def to_tp(k):
+        return remote(cots.at[tp], cots.at[tp], tp_send.at[k], tp_recv.at[k], at_tp(k))
+
+    for k in range(1, length):
+        to_line(k).start()
+    pl.when(z < length - 1)(lambda: to_up(hidden, z).start())
+    pl.when(z > 0)(lambda: to_down(hidden, z).start())
+    weights = remote(weight, peer, w_send, w_recv, pair)
+    weights.start()
+    keep_hidden = pltpu.make_async_copy(hidden, hid.at[z], own.at[0])
+    keep_hidden.start()
+    mine = pl.ds(pl.multiple_of(z * wide, wide), wide)
+    keep_cot = pltpu.make_async_copy(cot.at[rows, mine], cots.at[tp, z], own.at[1])
+    keep_cot.start()
+
+    keep_cot.wait()
+    for k in range(1, length):
+        source = lax.rem(z + length - k, length)
+        remote(
+            cots.at[tp, source], cots.at[tp, source], line_send.at[k], line_recv.at[k], pair
+        ).wait_recv()
+    for k in range(1, n_tp):
+        to_tp(k).start()
+
+    def arrived(slot):
+        remote(hid.at[slot], hid.at[slot], w_send, hid_recv.at[slot], pair).wait_recv()
+
+    for k in range(1, length):
+        @pl.when(z >= k)
+        def _():
+            arrived(z - k)
+            pl.when(z < length - 1)(lambda: to_up(hid.at[z - k], z - k).start())
+
+        @pl.when(z + k < length)
+        def _():
+            arrived(z + k)
+            pl.when(z > 0)(lambda: to_down(hid.at[z + k], z + k).start())
+
+    for k in range(1, n_tp):
+        source = lax.rem(tp + n_tp - k, n_tp)
+        remote(cots.at[source], cots.at[source], tp_send.at[k], tp_recv.at[k], pair).wait_recv()
+    for k in range(1, length):
+        to_line(k).wait_send()
+    for k in range(1, n_tp):
+        to_tp(k).wait_send()
+    keep_hidden.wait()
+    weights.wait()
+    for slot in range(length):
+        pl.when((z >= slot) & (z < length - 1))(lambda: to_up(hid.at[slot], slot).wait_send())
+        pl.when((z <= slot) & (z > 0))(lambda: to_down(hid.at[slot], slot).wait_send())
+
+
+def opening(hidden, weight, cotangent):
+    n_fsdp, n_tp = lax.axis_size("fsdp"), lax.axis_size("tp")
+    length = n_fsdp // 2
+    tokens, units = hidden.shape
+    width = weight.shape[1]
+    dma = pltpu.SemaphoreType.DMA
+    anywhere = pl.BlockSpec(memory_space=pl.ANY)
+    return pl.pallas_call(
+        functools.partial(opening_kernel, n_fsdp, n_tp),
+        out_shape=[
+            jax.ShapeDtypeStruct((length, tokens, units), BF16),
+            jax.ShapeDtypeStruct(weight.shape, BF16),
+            jax.ShapeDtypeStruct((n_tp, length, tokens // n_tp, 2 * width), BF16),
+        ],
+        in_specs=[anywhere] * 3,
+        out_specs=[anywhere] * 3,
+        scratch_shapes=[
+            dma((length,)), dma((length,)), dma((length,)), dma, dma,
+            dma((length,)), dma((length,)), dma((n_tp,)), dma((n_tp,)), dma((2,)),
+        ],
+        compiler_params=pltpu.CompilerParams(collective_id=0, has_side_effects=True),
+    )(hidden, weight, cotangent)
 
 
 def body(hidden, cotangent, weight, prompt_hidden):
@@ -63,24 +190,19 @@
     def step_of(froms, by):
         return [(2 * a + b, 2 * (a + by) + b) for a in froms for b in range(2)]
 
-    part = tokens // n_tp
-    rows = lax.dynamic_slice_in_dim(cotangent, tp * part, part, 0)
-    rows = rows.reshape(part, length, 2 * width).transpose(1, 0, 2)
-    mine = jnp.stack(swap_blocks(rows, "fsdp", 2))
-    cot = gather_by_permutes(mine, "tp")
+    grouped, weight_peer, cot = opening(hidden, weight, cotangent)
     cot = cot.transpose(1, 0, 2, 3).reshape(length, tokens, 2 * width)
-    cot_first = cot[:, :, :width]
-    cot_second = cot[:, :, width:]
-    cot_own = jnp.where(x == 0, cot_first, cot_second)
-    cot_peer = jnp.where(x == 0, cot_second, cot_first)
-
-    weight_peer = lax.ppermute(weight, "fsdp", across)
-    line_hidden = line_gather(hidden, (length, z), step_of)
-
-    both = jnp.concatenate([weight, weight_peer], axis=1)
-    cot_both = jnp.concatenate([cot_own, cot_peer], axis=2)
+
+    both = jnp.where(
+        x == 0,
+        jnp.concatenate([weight, weight_peer], axis=1),
+        jnp.concatenate([weight_peer, weight], axis=1),
+    )
     terms = [
-        lax.dot_general(cot_both[k], both, (((1,), (1,)), ((), ())), preferred_element_type=F32)
+        lax.dot_general(
+            block_of(cot, (z + length - k) % length), both,
+            (((1,), (1,)), ((), ())), preferred_element_type=F32,
+        )
         for k in range(length)
     ]
     up = down = None
@@ -89,13 +211,18 @@
         if s > 1:
             send_up = send_up + up.astype(F32)
             send_down = send_down + down.astype(F32)
-        up = lax.ppermute(send_up.astype(BF16), "fsdp", step_of(range(0, s), 1))
-        down = lax.ppermute(
-            send_down.astype(BF16), "fsdp", step_of(range(length - s, length), -1)
-        )
+        send_up, send_down = lax.optimization_barrier(
+            (send_up.astype(BF16), send_down.astype(BF16))
+        )
+        if s == 1:
+            cot_later, send_up, send_down = lax.optimization_barrier((cot, send_up, send_down))
+        up = lax.ppermute(send_up, "fsdp", step_of(range(0, s), 1))
+        down = lax.ppermute(send_down, "fsdp", step_of(range(length - s, length), -1))
     grad_hidden = (terms[0] + up.astype(F32) + down.astype(F32)).astype(BF16)
 
-    grouped = jnp.stack(line_hidden)
+    cot_first, cot_second = cot_later[:, :, :width], cot_later[:, :, width:]
+    cot_own = jnp.where(x == 0, cot_first, cot_second)
+    cot_peer = jnp.where(x == 0, cot_second, cot_first)
 
     def gradient(cots):
         parts = jnp.einsum("gtf,gtd->gfd", grouped, cots, preferred_element_type=F32)
@@ -105,6 +232,7 @@
     grad_weight = gradient(cot_own) + other.astype(F32)
     new_weight = (weight.astype(F32) - factor * grad_weight).astype(BF16)
 
+    prompt_hidden, _ = lax.optimization_barrier((prompt_hidden, cot_later))
     line_prompt = jnp.stack(line_gather(prompt_hidden, (length, z), step_of))
     pair_prompt = lax.ppermute(line_prompt, "fsdp", across)
     all_prompt = jnp.stack([line_prompt, pair_prompt])

time: 554 us -> 465 us (0.84)
  waiting for transfers between devices: 366 us -> 168 us
  Pallas kernels: 0 us -> 149 us
  starting transfers between devices: 64.9 us -> 45.6 us
  local copies, waits for them, and re-layouts: 24.8 us -> 6.61 us
    pallas_call x0 -> x1, Pallas kernels: none -> 149 us  [opening(): pl.pallas_call(functools.partial(opening_kernel, n_fsdp, n_tp), out_shape...]
    ppermute x6 -> x3, waiting for transfers between devices: 116 us -> 24.1 us  [line_gather(): lax.ppermute(down[-1], 'fsdp', step_of(range(1, length - k + 1), -1))]
    ppermute x7 -> x6, waiting for transfers between devices: 86.4 us -> 0.02 us  [the longest x3 0.01 us: body(): lax.ppermute(send_down, 'fsdp', step_of(range(length - s, length), -1))]
    ppermute x1, waiting for transfers between devices: 0.01 us -> 62.3 us  [body(): pair_prompt = lax.ppermute(line_prompt, 'fsdp', across)]
    ppermute x1, waiting for transfers between devices: 55.3 us -> 0.01 us  [body(): other = lax.ppermute(gradient(cot_peer).astype(BF16), 'fsdp', across)]
    ppermute x6 -> x3, waiting for transfers between devices: 24.7 us -> 11.7 us  [gather_by_permutes(): lax.ppermute(block, axis, [(i, (i + k) % count) for i in range(count)])]
    unnamed x56 -> x32, local copies, waits for them, and re-layouts: 12.9 us -> 0.76 us
    ppermute x6 -> x3, waiting for transfers between devices: 15.9 us -> 3.91 us  [swap_blocks(): got.append(lax.ppermute(block_of(blocks, (me + k) % groups), axis, perm))]
  transfers between devices with their start and end apart: 40 -> 27, of which waited for: 19 -> 13; matrix products, arithmetic and copies ran while one was open for 19% -> 18% of each run, Pallas kernels for 0% -> 0%
where the time goes in v2:
time: 465 us
  waiting for transfers between devices  168 us (36%)
  Pallas kernels  149 us (32%)
  matrix products  63.6 us (14%)
  starting transfers between devices  45.6 us (10%)
  other arithmetic  31.4 us (7%)
  local copies, waits for them, and re-layouts  6.61 us (1%)
    pallas_call x1, Pallas kernels, opening(): pl.pallas_call(functools.partial(opening_kernel, n_fsdp, n_tp), out_shape...  149 us
    ppermute x1, waiting for transfers between devices, body(): pair_prompt = lax.ppermute(line_prompt, 'fsdp', across)  62.3 us
    ppermute x7, waiting for transfers between devices, body(): pieces.append(lax.ppermute(summed[a, k], 'fsdp', perm))  36.9 us
    dot_general x4, matrix products, body(): lax.dot_general(block_of(cot, (z + length - k) % length), both, (((1,), (...  34.1 us
    ppermute x3, waiting for transfers between devices, line_gather(): lax.ppermute(up[-1], 'fsdp', step_of(range(k - 1, length - 1), 1))  28.6 us
    ppermute x3, waiting for transfers between devices, line_gather(): lax.ppermute(down[-1], 'fsdp', step_of(range(1, length - k + 1), -1))  24.1 us
    dot_general x2, matrix products, gradient(): jnp.einsum('gtf,gtd->gfd', grouped, cots, preferred_element_type=F32)  23.7 us
    ppermute x3, starting transfers between devices, body(): up = lax.ppermute(send_up, 'fsdp', step_of(range(0, s), 1))  14.6 us
  transfers between devices with their start and end apart: 27, of which 13 were waited for; matrix products, arithmetic and copies ran while one was open for 18% of the time, Pallas kernels for 0%

profile of v2, /device:TPU:0, one launch (start us, length us, event | category | flops | bytes accessed | tf_op | source)
XLA Modules:
  0.0 464.8 jit_solution(13499589655024056385)
XLA Ops:
  0.7 148.9 %shard_map.67 = (bf16[4,256,3584]{2,1,0:T(8,128)(2,1)}, bf16[3584,640]{1,0:T(8,128)(2,1)}, bf16[4,4,64,1280]{3,2,1,0:T(8,128)(2,1)}) custom-call(bf16[256,3584]{1,0:T(8,128)(2,1)} %hidden.1, bf16[3584,640]{1,0:T(8,128)(2,1)} %weight.1, bf16[256,5120]{1,0:T(8,128)(2,1)} %cot.1), custom_call_target="tpu_custom_call" | custom-call | tf_op jit(solution)/shard_map/pallas_call | solution.py:161
  149.6 2.0 copy.11
  151.6 10.6 %fusion.32 = (bf16[256,3584]{1,0:T(8,128)(2,1)}, f32[256,3584]{1,0:T(8,128)}) fusion(bf16[3584,640]{1,0:T(8,128)(2,1)} %get-tuple-element.17, bf16[3584,640]{1,0:T(8,128)(2,1)} %weight.1, pred[]{:T(512)S(6)} %eq.17, bf16[4,256,1280]{2,1,0:T(8,128)(2,1)S(1)} %bitcast.96, s32[]{:T(128)S(6)} %select_n.135), kind=kOutput, calls=%fused_computation.78 | convolution fusion | flops 2391015424 | bytes 15335429 | tf_op jit(solution)/shard_map/dot_general | solution.py:202
  162.3 4.9 %fusion.31 = (bf16[256,3584]{1,0:T(8,128)(2,1)}, f32[256,3584]{1,0:T(8,128)}) fusion(bf16[3584,640]{1,0:T(8,128)(2,1)S(1)} %copy-done.4, bf16[3584,640]{1,0:T(8,128)(2,1)S(1)} %bitcast.92, pred[]{:T(512)S(6)} %eq.17, bf16[4,256,1280]{2,1,0:T(8,128)(2,1)S(1)} %bitcast.97, s32[]{:T(128)S(6)} %select_n.139), kind=kOutput, calls=%fused_computation.77 | convolution fusion | flops 2391015424 | bytes 15335429 | tf_op jit(solution)/shard_map/dot_general | solution.py:202
  167.1 1.9 collective-permute-start.1
  169.0 2.7 collective-permute-start
  171.7 2.2 collective-permute-start.7
  173.9 1.3 collective-permute-start.8
  175.2 11.3 %convert_reduce_fusion.1 = bf16[3584,640]{1,0:T(8,128)(2,1)} fusion(bf16[4,256,3584]{2,1,0:T(8,128)(2,1)} %get-tuple-element.26, pred[]{:T(512)S(6)} %eq.17, bf16[4,256,1280]{2,1,0:T(8,128)(2,1)S(1)} %bitcast.98), kind=kOutput, calls=%fused_computation.1 | convolution fusion | flops 4714332160 | bytes 14548993 | tf_op jit(solution)/shard_map/gtf,gtd->gfd/dot_general | solution.py:228
  186.5 1.5 collective-permute-start.6
  188.0 12.4 %convert_reduce_fusion = f32[3584,640]{1,0:T(8,128)} fusion(bf16[4,256,3584]{2,1,0:T(8,128)(2,1)} %get-tuple-element.26, pred[]{:T(512)S(6)} %eq.17, bf16[4,256,1280]{2,1,0:T(8,128)(2,1)S(1)} %bitcast.99), kind=kOutput, calls=%fused_computation | convolution fusion | flops 4723507200 | bytes 19136512 | tf_op jit(solution)/shard_map/gtf,gtd->gfd/dot_general | solution.py:228
  200.4 28.6 %collective-permute-done.7 = bf16[128,3584]{1,0:T(8,128)(2,1)} collective-permute-done((bf16[128,3584]{1,0:T(8,128)(2,1)}, bf16[128,3584]{1,0:T(8,128)(2,1)}, u32[]{:S(2)}, u32[]{:S(2)}) %collective-permute-start.7) | collective-permute-done | bytes 917536 | tf_op jit(solution)/shard_map/ppermute | solution.py:47
  229.0 0.7 collective-permute-start.11
  229.7 1.5 collective-permute-start.9
  231.2 10.8 %add_convert_fusion.3 = (bf16[256,3584]{1,0:T(8,128)(2,1)}, bf16[256,3584]{1,0:T(8,128)(2,1)}) fusion(bf16[256,3584]{1,0:T(8,128)(2,1)} %collective-permute-done.1, bf16[256,3584]{1,0:T(8,128)(2,1)} %collective-permute-done, bf16[3584,640]{1,0:T(8,128)(2,1)} %get-tuple-element.17, bf16[3584,640]{1,0:T(8,128)(2,1)} %weight.1, pred[]{:T(512)S(6)} %eq.17, ...), kind=kOutput, calls=%fused_computation.9 | convolution fusion | flops 2395602944 | bytes 17170436 | tf_op jit(solution)/shard_map/dot_general | solution.py:202
  242.0 5.7 %collective-permute-start.2 = (bf16[256,3584]{1,0:T(8,128)(2,1)}, bf16[256,3584]{1,0:T(8,128)(2,1)S(1)}, u32[]{:S(2)}, u32[]{:S(2)}) collective-permute-start(bf16[256,3584]{1,0:T(8,128)(2,1)} %get-tuple-element.22), channel_id=1, source_target_pairs={{0,8},{4,12},{8,16},{12,20},{1,9},{5,13},{9,17},{13,21},{2,10},{6,... | collective-permute-start | bytes 5505032 | tf_op jit(solution)/shard_map/ppermute | solution.py:219
  247.8 0.7 collective-permute-start.12
  248.5 5.1 %collective-permute-done.9 = bf16[128,3584]{1,0:T(8,128)(2,1)S(1)} collective-permute-done((bf16[128,3584]{1,0:T(8,128)(2,1)}, bf16[128,3584]{1,0:T(8,128)(2,1)S(1)}, u32[]{:S(2)}, u32[]{:S(2)}) %collective-permute-start.9) | collective-permute-done | bytes 917536 | tf_op jit(solution)/shard_map/ppermute | solution.py:48
  253.7 1.3 collective-permute-start.10
  255.0 0.1 select_bitcast_fusion.1
  255.1 1.5 select_bitcast_fusion
  256.6 18.9 %collective-permute-done.10 = bf16[128,3584]{1,0:T(8,128)(2,1)S(1)} collective-permute-done((bf16[128,3584]{1,0:T(8,128)(2,1)S(1)}, bf16[128,3584]{1,0:T(8,128)(2,1)S(1)}, u32[]{:S(2)}, u32[]{:S(2)}) %collective-permute-start.10) | collective-permute-done | bytes 917536 | tf_op jit(solution)/shard_map/ppermute | solution.py:48
  275.5 0.1 select_bitcast_fusion.2
  275.6 4.3 fusion.30
  280.0 1.5 collective-permute-start.13
  281.5 7.8 %fusion.17 = f32[256,3584]{1,0:T(8,128)} fusion(bf16[4,256,1280]{2,1,0:T(8,128)(2,1)S(1)} %bitcast.101, s32[]{:T(128)S(6)} %select_n.130, bf16[3584,640]{1,0:T(8,128)(2,1)} %get-tuple-element.17, bf16[3584,640]{1,0:T(8,128)(2,1)S(1)} %bitcast.94, pred[]{:T(512)S(6)} %eq.17), kind=kOutput, calls=%fused_computation.35 | convolution fusion | flops 2390097920 | bytes 13500421 | tf_op jit(solution)/shard_map/dot_general | solution.py:202
  289.2 1.9 collective-permute-start.3
  291.2 1.6 add_convert_fusion.2
  292.8 10.1 %subtract_convert_fusion = bf16[3584,640]{1,0:T(8,128)(2,1)} fusion(f32[3584,640]{1,0:T(8,128)} %convert_reduce_fusion, bf16[3584,640]{1,0:T(8,128)(2,1)} %collective-permute-done.6, bf16[3584,640]{1,0:T(8,128)(2,1)} %weight.1), kind=kLoop, calls=%fused_computation.3 | loop fusion | flops 13762560 | bytes 22937600 | tf_op jit(solution)/shard_map/convert_element_type | solution.py:233
  302.9 62.3 %collective-permute-done.13 = bf16[4,128,3584]{2,1,0:T(8,128)(2,1)} collective-permute-done((bf16[4,128,3584]{2,1,0:T(8,128)(2,1)}, bf16[4,128,3584]{2,1,0:T(8,128)(2,1)}, u32[]{:S(2)}, u32[]{:S(2)}) %collective-permute-start.13) | collective-permute-done | bytes 3670048 | tf_op jit(solution)/shard_map/ppermute | solution.py:237
  365.3 4.0 pad_maximum_fusion
  369.2 0.5 copy-done
  369.7 5.8 %convolution_convert_fusion = bf16[1024,640]{1,0:T(8,128)(2,1)S(1)} fusion(bf16[1024,3584]{1,0:T(8,128)(2,1)S(1)} %bitcast.95, bf16[3584,640]{1,0:T(8,128)(2,1)S(1)} %copy-done), kind=kOutput, calls=%fused_computation.11 | convolution fusion | flops 4698275840 | bytes 13238272 | tf_op jit(solution)/shard_map/dot_general | solution.py:239
  375.6 0.1 dynamic-slice_bitcast_fusion.2
  375.8 0.1 collective-permute-start.15
  375.8 0.4 collective-permute-start.14
  376.3 3.1 add_convert_fusion.1
  379.4 1.5 collective-permute-start.5
  380.9 6.2 %collective-permute-start.4 = (bf16[256,3584]{1,0:T(8,128)(2,1)S(1)}, bf16[256,3584]{1,0:T(8,128)(2,1)}, u32[]{:S(2)}, u32[]{:S(2)}) collective-permute-start(bf16[256,3584]{1,0:T(8,128)(2,1)S(1)} %copy-done.3), channel_id=1, source_target_pairs={{0,8},{4,12},{8,16},{12,20},{16,24},{20,28},{1,9},{5,13},{9,17},{1... | collective-permute-start | bytes 5505032 | tf_op jit(solution)/shard_map/ppermute | solution.py:219
  387.1 3.6 collective-permute-done.15
  390.7 0.3 collective-permute-done.14
  391.0 0.2 fusion.10
  391.2 5.1 %collective-permute-start.17 = (bf16[32,640]{1,0:T(8,128)(2,1)S(1)}, bf16[32,640]{1,0:T(8,128)(2,1)S(1)}, u32[]{:S(2)}, u32[]{:S(2)}) collective-permute-start(bf16[32,640]{1,0:T(8,128)(2,1)S(1)} %get-tuple-element.42), channel_id=1, source_target_pairs={{0,24},{4,28},{8,0},{12,4},{16,8},{20,12},{24,16},{28,20},{1,25},{... | collective-permute-start | bytes 122888 | tf_op jit(solution)/shard_map/ppermute | solution.py:257
  396.3 0.6 collective-permute-start.19
  397.0 29.4 %collective-permute-done.17 = bf16[32,640]{1,0:T(8,128)(2,1)S(1)} collective-permute-done((bf16[32,640]{1,0:T(8,128)(2,1)S(1)}, bf16[32,640]{1,0:T(8,128)(2,1)S(1)}, u32[]{:S(2)}, u32[]{:S(2)}) %collective-permute-start.17) | collective-permute-done | bytes 40992 | tf_op jit(solution)/shard_map/ppermute | solution.py:257
  426.4 1.5 collective-permute-start.20
  427.9 1.3 collective-permute-done.18
  429.2 5.0 %collective-permute-start.21 = (bf16[32,640]{1,0:T(8,128)(2,1)S(1)}, bf16[32,640]{1,0:T(8,128)(2,1)S(1)}, u32[]{:S(2)}, u32[]{:S(2)}) collective-permute-start(bf16[32,640]{1,0:T(8,128)(2,1)S(1)} %get-tuple-element.38), channel_id=1, source_target_pairs={{0,28},{4,24},{8,4},{12,0},{16,12},{20,8},{24,20},{28,16},{1,29},{... | collective-permute-start | bytes 122888 | tf_op jit(solution)/shard_map/ppermute | solution.py:257
  434.3 0.6 collective-permute-start.23
  434.9 1.2 collective-permute-done.21
  436.1 4.4 collective-permute-done.22
  440.5 0.5 collective-permute-done.23
  441.1 0.3 copy.15
  441.4 1.7 rev.3
  443.2 0.4 broadcast_select_fusion
  443.6 0.8 fusion.24
  444.5 0.2 reshape.42
  444.8 5.0 %add_convert_fusion = bf16[256,3584]{1,0:T(8,128)(2,1)} fusion(bf16[256,3584]{1,0:T(8,128)(2,1)} %collective-permute-done.5, f32[256,3584]{1,0:T(8,128)} %fusion.17, bf16[256,3584]{1,0:T(8,128)(2,1)} %collective-permute-done.4), kind=kLoop, calls=%fused_computation.6 | loop fusion | flops 4587520 | bytes 9175040 | tf_op jit(solution)/shard_map/convert_element_type | solution.py:221
  449.8 1.4 collective-permute-start.25
  451.2 0.2 collective-permute-start.26
  451.4 0.2 stack_reshape.4
  451.7 8.7 %collective-permute-done.25 = bf16[32,5120]{1,0:T(8,128)(2,1)S(1)} collective-permute-done((bf16[32,5120]{1,0:T(8,128)(2,1)S(1)}, bf16[32,5120]{1,0:T(8,128)(2,1)S(1)}, u32[]{:S(2)}, u32[]{:S(2)}) %collective-permute-start.25) | collective-permute-done | bytes 327712 | tf_op jit(solution)/shard_map/ppermute | solution.py:39
  460.4 3.1 collective-permute-done.26
  463.6 1.2 constant_dynamic-slice_fusion
  (54 shorter events, 0.6 us)
Async XLA Ops:
  149.6 12.6 %slice-start = ((s8[4587520]{0:T(1024)(128)(4,1)}), s8[393216]{0:T(1024)(128)(4,1)S(1)}, s32[]{:S(2)}) async-start(s8[4587520]{0:T(1024)(128)(4,1)} %bitcast.91), calls=%async_computation | async-start | bytes 786432
  151.6 10.7 %slice-start.1 = ((s8[4587520]{0:T(1024)(128)(4,1)}), s8[4194304]{0:T(1024)(128)(4,1)S(1)}, s32[]{:S(2)}) async-start(s8[4587520]{0:T(1024)(128)(4,1)} %bitcast.91), calls=%async_computation.1 | async-start | bytes 8388608
  151.6 10.6 %copy-start.4 = (bf16[3584,640]{1,0:T(8,128)(2,1)S(1)}, bf16[3584,640]{1,0:T(8,128)(2,1)}, u32[]{:S(2)}) copy-start(bf16[3584,640]{1,0:T(8,128)(2,1)} %get-tuple-element.17) | copy-start | bytes 13762564
  167.1 64.1 %collective-permute-start.1 = (bf16[256,3584]{1,0:T(8,128)(2,1)}, bf16[256,3584]{1,0:T(8,128)(2,1)}, u32[]{:S(2)}, u32[]{:S(2)}) collective-permute-start(bf16[256,3584]{1,0:T(8,128)(2,1)} %get-tuple-element.21), channel_id=1, source_target_pairs={{24,16},{28,20},{25,17},{29,21},{26,18},{30,22},{27,19},{31,23}} | collective-permute-start | bytes 5505032 | tf_op jit(solution)/shard_map/ppermute | solution.py:220
  169.0 62.2 %collective-permute-start = (bf16[256,3584]{1,0:T(8,128)(2,1)}, bf16[256,3584]{1,0:T(8,128)(2,1)}, u32[]{:S(2)}, u32[]{:S(2)}) collective-permute-start(bf16[256,3584]{1,0:T(8,128)(2,1)} %get-tuple-element.20), channel_id=1, source_target_pairs={{0,8},{4,12},{1,9},{5,13},{2,10},{6,14},{3,11},{7,15}} | collective-permute-start | bytes 5505032 | tf_op jit(solution)/shard_map/ppermute | solution.py:219
  171.7 57.3 %collective-permute-start.7 = (bf16[128,3584]{1,0:T(8,128)(2,1)}, bf16[128,3584]{1,0:T(8,128)(2,1)}, u32[]{:S(2)}, u32[]{:S(2)}) collective-permute-start(bf16[128,3584]{1,0:T(8,128)(2,1)} %param.7), channel_id=1, source_target_pairs={{0,8},{4,12},{8,16},{12,20},{16,24},{20,28},{1,9},{5,13},{9,17},{1... | collective-permute-start | bytes 2752520 | tf_op jit(solution)/shard_map/ppermute | solution.py:47
  173.9 55.8 %collective-permute-start.8 = (bf16[128,3584]{1,0:T(8,128)(2,1)}, bf16[128,3584]{1,0:T(8,128)(2,1)}, u32[]{:S(2)}, u32[]{:S(2)}) collective-permute-start(bf16[128,3584]{1,0:T(8,128)(2,1)} %param.7), channel_id=1, source_target_pairs={{8,0},{12,4},{16,8},{20,12},{24,16},{28,20},{9,1},{13,5},{17,9},{2... | collective-permute-start | bytes 2752520 | tf_op jit(solution)/shard_map/ppermute | solution.py:48
  186.5 106.3 %collective-permute-start.6 = (bf16[3584,640]{1,0:T(8,128)(2,1)}, bf16[3584,640]{1,0:T(8,128)(2,1)}, u32[]{:S(2)}, u32[]{:S(2)}) collective-permute-start(bf16[3584,640]{1,0:T(8,128)(2,1)} %convert_reduce_fusion.1), channel_id=1, source_target_pairs={{0,4},{4,0},{8,12},{12,8},{16,20},{20,16},{24,28},{28,24},{1,5},{5... | collective-permute-start | bytes 13762568 | tf_op jit(solution)/shard_map/ppermute | solution.py:231
  229.0 18.8 %collective-permute-start.11 = (bf16[128,3584]{1,0:T(8,128)(2,1)}, bf16[128,3584]{1,0:T(8,128)(2,1)S(1)}, u32[]{:S(2)}, u32[]{:S(2)}) collective-permute-start(bf16[128,3584]{1,0:T(8,128)(2,1)} %collective-permute-done.7), channel_id=1, source_target_pairs={{8,16},{12,20},{16,24},{20,28},{9,17},{13,21},{17,25},{21,29},{10,... | collective-permute-start | bytes 2752520 | tf_op jit(solution)/shard_map/ppermute | solution.py:47
  229.7 24.0 %collective-permute-start.9 = (bf16[128,3584]{1,0:T(8,128)(2,1)}, bf16[128,3584]{1,0:T(8,128)(2,1)S(1)}, u32[]{:S(2)}, u32[]{:S(2)}) collective-permute-start(bf16[128,3584]{1,0:T(8,128)(2,1)} %collective-permute-done.8), channel_id=1, source_target_pairs={{8,0},{12,4},{16,8},{20,12},{9,1},{13,5},{17,9},{21,13},{10,2},{14... | collective-permute-start | bytes 2752520 | tf_op jit(solution)/shard_map/ppermute | solution.py:48
  242.0 49.1 %collective-permute-start.2 = (bf16[256,3584]{1,0:T(8,128)(2,1)}, bf16[256,3584]{1,0:T(8,128)(2,1)S(1)}, u32[]{:S(2)}, u32[]{:S(2)}) collective-permute-start(bf16[256,3584]{1,0:T(8,128)(2,1)} %get-tuple-element.22), channel_id=1, source_target_pairs={{0,8},{4,12},{8,16},{12,20},{1,9},{5,13},{9,17},{13,21},{2,10},{6,... | collective-permute-start | bytes 5505032 | tf_op jit(solution)/shard_map/ppermute | solution.py:219
  247.8 7.3 %collective-permute-start.12 = (bf16[128,3584]{1,0:T(8,128)(2,1)S(1)}, bf16[128,3584]{1,0:T(8,128)(2,1)S(1)}, u32[]{:S(2)}, u32[]{:S(2)}) collective-permute-start(bf16[128,3584]{1,0:T(8,128)(2,1)S(1)} %collective-permute-done.11), channel_id=1, source_target_pairs={{16,24},{20,28},{17,25},{21,29},{18,26},{22,30},{19,27},{23,31}} | collective-permute-start | bytes 2752520 | tf_op jit(solution)/shard_map/ppermute | solution.py:47
  253.7 21.8 %collective-permute-start.10 = (bf16[128,3584]{1,0:T(8,128)(2,1)S(1)}, bf16[128,3584]{1,0:T(8,128)(2,1)S(1)}, u32[]{:S(2)}, u32[]{:S(2)}) collective-permute-start(bf16[128,3584]{1,0:T(8,128)(2,1)S(1)} %collective-permute-done.9), channel_id=1, source_target_pairs={{8,0},{12,4},{9,1},{13,5},{10,2},{14,6},{11,3},{15,7}} | collective-permute-start | bytes 2752520 | tf_op jit(solution)/shard_map/ppermute | solution.py:48
  255.1 26.4 %slice-start.2 = ((s8[4587520]{0:T(1024)(128)(4,1)}), s8[4194304]{0:T(1024)(128)(4,1)S(1)}, s32[]{:S(2)}) async-start(s8[4587520]{0:T(1024)(128)(4,1)} %bitcast.93), calls=%async_computation.2 | async-start | bytes 8388608
  275.6 5.9 %slice-start.3 = ((s8[4587520]{0:T(1024)(128)(4,1)}), s8[393216]{0:T(1024)(128)(4,1)S(1)}, s32[]{:S(2)}) async-start(s8[4587520]{0:T(1024)(128)(4,1)} %bitcast.93), calls=%async_computation.3 | async-start | bytes 786432
  280.0 11.2 %copy-start.2 = (f32[256,3584]{1,0:T(8,128)S(1)}, f32[256,3584]{1,0:T(8,128)}, u32[]{:S(2)}) copy-start(f32[256,3584]{1,0:T(8,128)} %get-tuple-element.46) | copy-start | bytes 11010052
  280.0 85.3 %collective-permute-start.13 = (bf16[4,128,3584]{2,1,0:T(8,128)(2,1)}, bf16[4,128,3584]{2,1,0:T(8,128)(2,1)}, u32[]{:S(2)}, u32[]{:S(2)}) collective-permute-start(bf16[4,128,3584]{2,1,0:T(8,128)(2,1)} %get-tuple-element.30), channel_id=1, source_target_pairs={{0,4},{4,0},{8,12},{12,8},{16,20},{20,16},{24,28},{28,24},{1,5},{5... | collective-permute-start | bytes 11010056 | tf_op jit(solution)/shard_map/ppermute | solution.py:237
  289.2 87.0 %collective-permute-start.3 = (bf16[256,3584]{1,0:T(8,128)(2,1)}, bf16[256,3584]{1,0:T(8,128)(2,1)}, u32[]{:S(2)}, u32[]{:S(2)}) collective-permute-start(bf16[256,3584]{1,0:T(8,128)(2,1)} %get-tuple-element.23), channel_id=1, source_target_pairs={{16,8},{20,12},{24,16},{28,20},{17,9},{21,13},{25,17},{29,21},{18,... | collective-permute-start | bytes 5505032 | tf_op jit(solution)/shard_map/ppermute | solution.py:220
  365.3 4.4 copy-start
  369.7 6.6 %copy-start.1 = (f32[256,3584]{1,0:T(8,128)S(1)}, f32[256,3584]{1,0:T(8,128)}, u32[]{:S(2)}) copy-start(f32[256,3584]{1,0:T(8,128)} %get-tuple-element.44) | copy-start | bytes 11010052
  375.6 5.4 %copy-start.3 = (bf16[256,3584]{1,0:T(8,128)(2,1)S(1)}, bf16[256,3584]{1,0:T(8,128)(2,1)}, u32[]{:S(2)}) copy-start(bf16[256,3584]{1,0:T(8,128)(2,1)} %add_convert_fusion.2) | copy-start | bytes 5505028
  375.7 11.4 %collective-permute-start.16 = (bf16[8,32,640]{2,1,0:T(8,128)(2,1)S(1)}, bf16[8,32,640]{2,1,0:T(8,128)(2,1)S(1)}, u32[]{:S(2)}, u32[]{:S(2)}) collective-permute-start(bf16[8,32,640]{2,1,0:T(8,128)(2,1)S(1)} %get-tuple-element.34), channel_id=1, source_target_pairs={{0,3},{1,0},{2,1},{3,2},{4,7},{5,4},{6,5},{7,6},{8,11},{9,8},{10,9... | collective-permute-start | bytes 983048 | tf_op jit(solution)/shard_map/ppermute | solution.py:25
  375.8 14.9 %collective-permute-start.15 = (bf16[8,32,640]{2,1,0:T(8,128)(2,1)S(1)}, bf16[8,32,640]{2,1,0:T(8,128)(2,1)S(1)}, u32[]{:S(2)}, u32[]{:S(2)}) collective-permute-start(bf16[8,32,640]{2,1,0:T(8,128)(2,1)S(1)} %get-tuple-element.35), channel_id=1, source_target_pairs={{0,2},{1,3},{2,0},{3,1},{4,6},{5,7},{6,4},{7,5},{8,10},{9,11},{10,... | collective-permute-start | bytes 983048 | tf_op jit(solution)/shard_map/ppermute | solution.py:25
  375.8 15.2 %collective-permute-start.14 = (bf16[8,32,640]{2,1,0:T(8,128)(2,1)S(1)}, bf16[8,32,640]{2,1,0:T(8,128)(2,1)S(1)}, u32[]{:S(2)}, u32[]{:S(2)}) collective-permute-start(bf16[8,32,640]{2,1,0:T(8,128)(2,1)S(1)} %get-tuple-element.33), channel_id=1, source_target_pairs={{0,1},{1,2},{2,3},{3,0},{4,5},{5,6},{6,7},{7,4},{8,9},{9,10},{10,1... | collective-permute-start | bytes 983048 | tf_op jit(solution)/shard_map/ppermute | solution.py:25
  379.4 65.4 %collective-permute-start.5 = (bf16[256,3584]{1,0:T(8,128)(2,1)}, bf16[256,3584]{1,0:T(8,128)(2,1)}, u32[]{:S(2)}, u32[]{:S(2)}) collective-permute-start(bf16[256,3584]{1,0:T(8,128)(2,1)} %add_convert_fusion.1), channel_id=1, source_target_pairs={{8,0},{12,4},{16,8},{20,12},{24,16},{28,20},{9,1},{13,5},{17,9},{2... | collective-permute-start | bytes 5505032 | tf_op jit(solution)/shard_map/ppermute | solution.py:220
  380.9 63.9 %collective-permute-start.4 = (bf16[256,3584]{1,0:T(8,128)(2,1)S(1)}, bf16[256,3584]{1,0:T(8,128)(2,1)}, u32[]{:S(2)}, u32[]{:S(2)}) collective-permute-start(bf16[256,3584]{1,0:T(8,128)(2,1)S(1)} %copy-done.3), channel_id=1, source_target_pairs={{0,8},{4,12},{8,16},{12,20},{16,24},{20,28},{1,9},{5,13},{9,17},{1... | collective-permute-start | bytes 5505032 | tf_op jit(solution)/shard_map/ppermute | solution.py:219
  391.2 35.2 %collective-permute-start.17 = (bf16[32,640]{1,0:T(8,128)(2,1)S(1)}, bf16[32,640]{1,0:T(8,128)(2,1)S(1)}, u32[]{:S(2)}, u32[]{:S(2)}) collective-permute-start(bf16[32,640]{1,0:T(8,128)(2,1)S(1)} %get-tuple-element.42), channel_id=1, source_target_pairs={{0,24},{4,28},{8,0},{12,4},{16,8},{20,12},{24,16},{28,20},{1,25},{... | collective-permute-start | bytes 122888 | tf_op jit(solution)/shard_map/ppermute | solution.py:257
  396.3 32.9 %collective-permute-start.18 = (bf16[32,640]{1,0:T(8,128)(2,1)S(1)}, bf16[32,640]{1,0:T(8,128)(2,1)S(1)}, u32[]{:S(2)}, u32[]{:S(2)}) collective-permute-start(bf16[32,640]{1,0:T(8,128)(2,1)S(1)} %get-tuple-element.41), channel_id=1, source_target_pairs={{0,16},{4,20},{8,24},{12,28},{16,0},{20,4},{24,8},{28,12},{1,17},{... | collective-permute-start | bytes 122888 | tf_op jit(solution)/shard_map/ppermute | solution.py:257
  396.3 37.9 %collective-permute-start.19 = (bf16[32,640]{1,0:T(8,128)(2,1)S(1)}, bf16[32,640]{1,0:T(8,128)(2,1)S(1)}, u32[]{:S(2)}, u32[]{:S(2)}) collective-permute-start(bf16[32,640]{1,0:T(8,128)(2,1)S(1)} %get-tuple-element.40), channel_id=1, source_target_pairs={{0,8},{4,12},{8,16},{12,20},{16,24},{20,28},{24,0},{28,4},{1,9},{5... | collective-permute-start | bytes 122888 | tf_op jit(solution)/shard_map/ppermute | solution.py:257
  426.4 7.9 %collective-permute-start.20 = (bf16[32,640]{1,0:T(8,128)(2,1)S(1)}, bf16[32,640]{1,0:T(8,128)(2,1)S(1)}, u32[]{:S(2)}, u32[]{:S(2)}) collective-permute-start(bf16[32,640]{1,0:T(8,128)(2,1)S(1)} %get-tuple-element.39), channel_id=1, source_target_pairs={{0,4},{4,0},{8,12},{12,8},{16,20},{20,16},{24,28},{28,24},{1,5},{5... | collective-permute-start | bytes 122888 | tf_op jit(solution)/shard_map/ppermute | solution.py:257
  429.2 6.9 %collective-permute-start.21 = (bf16[32,640]{1,0:T(8,128)(2,1)S(1)}, bf16[32,640]{1,0:T(8,128)(2,1)S(1)}, u32[]{:S(2)}, u32[]{:S(2)}) collective-permute-start(bf16[32,640]{1,0:T(8,128)(2,1)S(1)} %get-tuple-element.38), channel_id=1, source_target_pairs={{0,28},{4,24},{8,4},{12,0},{16,12},{20,8},{24,20},{28,16},{1,29},{... | collective-permute-start | bytes 122888 | tf_op jit(solution)/shard_map/ppermute | solution.py:257
  434.2 6.3 %collective-permute-start.22 = (bf16[32,640]{1,0:T(8,128)(2,1)S(1)}, bf16[32,640]{1,0:T(8,128)(2,1)S(1)}, u32[]{:S(2)}, u32[]{:S(2)}) collective-permute-start(bf16[32,640]{1,0:T(8,128)(2,1)S(1)} %get-tuple-element.37), channel_id=1, source_target_pairs={{0,20},{4,16},{8,28},{12,24},{16,4},{20,0},{24,12},{28,8},{1,21},{... | collective-permute-start | bytes 122888 | tf_op jit(solution)/shard_map/ppermute | solution.py:257
  434.3 6.8 %collective-permute-start.23 = (bf16[32,640]{1,0:T(8,128)(2,1)S(1)}, bf16[32,640]{1,0:T(8,128)(2,1)S(1)}, u32[]{:S(2)}, u32[]{:S(2)}) collective-permute-start(bf16[32,640]{1,0:T(8,128)(2,1)S(1)} %get-tuple-element.36), channel_id=1, source_target_pairs={{0,12},{4,8},{8,20},{12,16},{16,28},{20,24},{24,4},{28,0},{1,13},{... | collective-permute-start | bytes 122888 | tf_op jit(solution)/shard_map/ppermute | solution.py:257
  444.7 6.9 %collective-permute-start.24 = (bf16[32,5120]{1,0:T(8,128)(2,1)S(1)}, bf16[32,5120]{1,0:T(8,128)(2,1)S(1)}, u32[]{:S(2)}, u32[]{:S(2)}) collective-permute-start(bf16[32,5120]{1,0:T(8,128)(2,1)S(1)} %reshape.42), channel_id=1, source_target_pairs={{0,3},{1,0},{2,1},{3,2},{4,7},{5,4},{6,5},{7,6},{8,11},{9,8},{10,9... | collective-permute-start | bytes 983048 | tf_op jit(solution)/shard_map/ppermute | solution.py:39
  449.8 10.5 %collective-permute-start.25 = (bf16[32,5120]{1,0:T(8,128)(2,1)S(1)}, bf16[32,5120]{1,0:T(8,128)(2,1)S(1)}, u32[]{:S(2)}, u32[]{:S(2)}) collective-permute-start(bf16[32,5120]{1,0:T(8,128)(2,1)S(1)} %reshape.42), channel_id=1, source_target_pairs={{0,2},{1,3},{2,0},{3,1},{4,6},{5,7},{6,4},{7,5},{8,10},{9,11},{10,... | collective-permute-start | bytes 983048 | tf_op jit(solution)/shard_map/ppermute | solution.py:39
  451.2 12.2 %collective-permute-start.26 = (bf16[32,5120]{1,0:T(8,128)(2,1)S(1)}, bf16[32,5120]{1,0:T(8,128)(2,1)S(1)}, u32[]{:S(2)}, u32[]{:S(2)}) collective-permute-start(bf16[32,5120]{1,0:T(8,128)(2,1)S(1)} %reshape.42), channel_id=1, source_target_pairs={{0,1},{1,2},{2,3},{3,0},{4,5},{5,6},{6,7},{7,4},{8,9},{9,10},{10,1... | collective-permute-start | bytes 983048 | tf_op jit(solution)/shard_map/ppermute | solution.py:39
